TPU v7x, 512 devices: a whole 4x8x8 slice. The times are simulated.
512 devices in a mesh: grp: 32 (over x, z_lo, core), sp: 16 (over y, z_hi).
Axes of the slice: x: 4, y: 8, z: 8 (z_hi: 2, z_lo: 4; z = z_hi * 4 + z_lo), core: 2. Of those that a mesh axis runs over, the one named last changes fastest.
Arguments:
- queries: bfloat16 [65536, 4096], P(('grp', 'sp')), may hold values from -60 to 60
- keys: bfloat16 [65536, 512], P(('grp', 'sp')), may hold values from -60 to 60
- values: bfloat16 [65536, 512], P(('grp', 'sp')), may hold values from -6 to 6
- grad_out: bfloat16 [65536, 4096], P(('grp', 'sp')), may hold values from -40 to 40
- gain_q: float32 [128], replicated, may hold values from 0.5 to 6
- gain_k: float32 [128], replicated, may hold values from 0.5 to 6
- doc_ids: int32 [65536], P(('grp', 'sp')), may hold values from 0 to 1023, never falling along the last dimension, each value on 1 to 128 neighbouring positions
- bucket_len: int32 [32], P('grp'), may hold values from 512 to 2048, as said below
Outputs:
- grad_queries: bfloat16 [65536, 4096], P(('grp', 'sp'))
- grad_keys: bfloat16 [65536, 512], P(('grp', 'sp'))
- grad_values: bfloat16 [65536, 512], P(('grp', 'sp'))
- grad_gain_q: float32 [128], replicated
- grad_gain_k: float32 [128], replicated
Inputs may be any that keep to these rules, and one draw needn't show every extreme that they name: `doc_ids`: ids never fall along the tokens; a document has at most 128 tokens and may run across buckets. Slots at positions from bucket_len on are padding. Some bucket is full and some holds 512 tokens.
All inputs are finite; a program needn't handle non-finite values.
Results may differ from a plain program's by a relative error of at most 0.006.
The roundings to bfloat16 on the way count: a program that leaves them out, or rounds other values in their place, can miss the bound.
Values may be sent and summed in bfloat16 or wider, within the bound.
A program may use at most 128 MiB of HBM per device.

v0:
```python
import jax
import jax.numpy as jnp
from jax import lax
from jax.sharding import PartitionSpec as P

norm_eps = 1e-06
masked_score = -1e30


def rms_factor(inputs):
    return lax.rsqrt(jnp.mean(inputs * inputs, axis=-1, keepdims=True) + norm_eps)


def norm_backward(inputs, factor, gain, upstream):
    scaled = gain * upstream
    inner_mean = jnp.mean(scaled * inputs, axis=-1, keepdims=True)
    return factor * scaled - inputs * factor * factor * factor * inner_mean


def windows(padded, row_start, block_rows, tile):
    slab = padded[row_start : row_start + block_rows + tile]
    tiles = block_rows // tile
    lower = slab[:block_rows].reshape((tiles, tile) + slab.shape[1:])
    upper = slab[tile:].reshape((tiles, tile) + slab.shape[1:])
    return jnp.concatenate([lower, upper], axis=1)


def block_grads(
    query_norm,
    grad_head,
    key_pad,
    value_pad,
    segment_pad,
    bucket_end,
    row_start,
    block_rows,
    tile,
    score_scale,
):
    tiles = block_rows // tile
    head_dim = query_norm.shape[1]
    query_part = query_norm[row_start : row_start + block_rows].reshape(tiles, tile, head_dim)
    grad_part = grad_head[row_start : row_start + block_rows].reshape(tiles, tile, head_dim)
    key_part = windows(key_pad, row_start, block_rows, tile)
    value_part = windows(value_pad, row_start, block_rows, tile)
    key_ids = windows(segment_pad, row_start, block_rows, tile)
    query_ids = segment_pad[tile + row_start : tile + row_start + block_rows].reshape(tiles, tile)
    query_places = row_start + jnp.arange(block_rows, dtype=jnp.int32).reshape(tiles, tile)
    key_places = (
        row_start
        - tile
        + jnp.arange(tiles, dtype=jnp.int32)[:, None] * tile
        + jnp.arange(2 * tile, dtype=jnp.int32)[None, :]
    )
    allowed = (query_ids[:, :, None] == key_ids[:, None, :]) & (
        key_places[:, None, :] <= query_places[:, :, None]
    )
    live_rows = (query_places < bucket_end).astype(jnp.float32)[:, :, None]
    scores = (
        jnp.einsum("nqd,nkd->nqk", query_part, key_part, preferred_element_type=jnp.float32)
        * score_scale
    )
    scores = jnp.where(allowed, scores, masked_score)
    highest = jnp.max(scores, axis=-1, keepdims=True)
    weights = jnp.exp(scores - highest)
    attention = weights / jnp.sum(weights, axis=-1, keepdims=True) * live_rows
    grad_attention = jnp.einsum(
        "nqd,nkd->nqk", grad_part, value_part, preferred_element_type=jnp.float32
    )
    row_delta = jnp.sum(attention * grad_attention, axis=-1, keepdims=True)
    grad_scores = (attention * (grad_attention - row_delta)).astype(jnp.bfloat16)
    attention_low = attention.astype(jnp.bfloat16)
    query_grad = (
        jnp.einsum(
            "nqk,nkd->nqd", grad_scores, key_part, preferred_element_type=jnp.float32
        ).reshape(block_rows, head_dim)
        * score_scale
    )
    key_add = (
        jnp.einsum("nqk,nqd->nkd", grad_scores, query_part, preferred_element_type=jnp.float32)
        * score_scale
    )
    value_add = jnp.einsum(
        "nqk,nqd->nkd", attention_low, grad_part, preferred_element_type=jnp.float32
    )
    return (
        query_grad,
        key_add[:, :tile].reshape(block_rows, head_dim),
        key_add[:, tile:].reshape(block_rows, head_dim),
        value_add[:, :tile].reshape(block_rows, head_dim),
        value_add[:, tile:].reshape(block_rows, head_dim),
    )


def join_halves(lowers, uppers, tile):
    lower_all = jnp.concatenate(lowers, axis=0)
    upper_all = jnp.concatenate(uppers, axis=0)
    shifted = jnp.concatenate(
        [lower_all[tile:], jnp.zeros((tile, lower_all.shape[1]), jnp.float32)], axis=0
    )
    return upper_all + shifted


def body(queries, keys, values, grad_out, gain_q, gain_k, doc_ids, bucket_len):
    row_count = queries.shape[0]
    head_dim = gain_q.shape[0]
    heads_q = queries.shape[1] // head_dim
    heads_k = keys.shape[1] // head_dim
    seq_devices = lax.axis_size("sp")
    local_heads = heads_q // seq_devices
    group_size = heads_q // heads_k
    bucket = row_count * seq_devices
    tile = min(128, bucket // 4)
    score_scale = head_dim ** (-0.5)
    query_heads, grad_heads = (
        lax.all_to_all(queries, "sp", split_axis=1, concat_axis=0, tiled=True),
        lax.all_to_all(grad_out, "sp", split_axis=1, concat_axis=0, tiled=True),
    )
    shared_head = lax.axis_index("sp") * local_heads // group_size
    key_all, value_all, segments = (
        lax.all_gather(keys, "sp", axis=0, tiled=True),
        lax.all_gather(values, "sp", axis=0, tiled=True),
        lax.all_gather(doc_ids, "sp", axis=0, tiled=True),
    )
    key_own = lax.dynamic_slice_in_dim(key_all, shared_head * head_dim, head_dim, 1)
    value_own = lax.dynamic_slice_in_dim(value_all, shared_head * head_dim, head_dim, 1)
    key_float = key_own.astype(jnp.float32)
    key_norm = (key_float * rms_factor(key_float) * gain_k).astype(jnp.bfloat16)
    key_pad = jnp.concatenate([jnp.zeros((tile, head_dim), jnp.bfloat16), key_norm], axis=0)
    value_pad = jnp.concatenate([jnp.zeros((tile, head_dim), jnp.bfloat16), value_own], axis=0)
    segment_pad = jnp.concatenate(
        [jnp.full((tile,), -1, jnp.int32), segments.astype(jnp.int32)], axis=0
    )
    bucket_end = bucket_len[0]
    block_rows = min(512, bucket)
    block_count = bucket // block_rows
    key_grad = jnp.zeros((bucket, head_dim), jnp.float32)
    value_grad = jnp.zeros((bucket, head_dim), jnp.float32)
    grad_columns = []
    gain_q_part = jnp.zeros((head_dim,), jnp.float32)
    for head_index in range(local_heads):
        query_float = query_heads[:, head_index * head_dim : (head_index + 1) * head_dim].astype(
            jnp.float32
        )
        query_factor = rms_factor(query_float)
        query_norm = (query_float * query_factor * gain_q).astype(jnp.bfloat16)
        grad_head = grad_heads[:, head_index * head_dim : (head_index + 1) * head_dim]
        query_grads = []
        key_lowers = []
        key_uppers = []
        value_lowers = []
        value_uppers = []
        for block_index in range(block_count):
            row_start = block_index * block_rows
            results = block_grads(
                query_norm,
                grad_head,
                key_pad,
                value_pad,
                segment_pad,
                bucket_end,
                row_start,
                block_rows,
                tile,
                score_scale,
            )
            query_grads.append(results[0])
            key_lowers.append(results[1])
            key_uppers.append(results[2])
            value_lowers.append(results[3])
            value_uppers.append(results[4])
        key_grad = key_grad + join_halves(key_lowers, key_uppers, tile)
        value_grad = value_grad + join_halves(value_lowers, value_uppers, tile)
        grad_qnorm = jnp.concatenate(query_grads, axis=0)
        grad_columns.append(
            norm_backward(query_float, query_factor, gain_q, grad_qnorm).astype(jnp.bfloat16)
        )
        gain_q_part = gain_q_part + jnp.sum(grad_qnorm * query_float * query_factor, axis=0)
    grad_local = jnp.concatenate(grad_columns, axis=1)
    grad_queries = lax.all_to_all(grad_local, "sp", split_axis=0, concat_axis=1, tiled=True)
    key_slots, value_slots = (
        lax.all_to_all(key_grad, "sp", split_axis=0, concat_axis=1, tiled=True),
        lax.all_to_all(value_grad, "sp", split_axis=0, concat_axis=1, tiled=True),
    )
    spread = seq_devices // heads_k
    grad_knorm = key_slots.reshape(row_count, heads_k, spread, head_dim).sum(axis=2)
    value_sum = value_slots.reshape(row_count, heads_k, spread, head_dim).sum(axis=2)
    grad_values = value_sum.reshape(row_count, heads_k * head_dim).astype(jnp.bfloat16)
    key_input = keys.reshape(row_count, heads_k, head_dim).astype(jnp.float32)
    key_factor = rms_factor(key_input)
    grad_keys = (
        norm_backward(key_input, key_factor, gain_k, grad_knorm)
        .reshape(row_count, heads_k * head_dim)
        .astype(jnp.bfloat16)
    )
    gain_k_part = jnp.sum(grad_knorm * key_input * key_factor, axis=(0, 1))
    gain_totals = lax.psum((gain_q_part, gain_k_part), ("grp", "sp"))
    total_scale = (row_count * seq_devices * lax.axis_size("grp")) ** (-0.5)
    return (
        grad_queries,
        grad_keys,
        grad_values,
        gain_totals[0] * total_scale,
        gain_totals[1] * total_scale,
    )


def solution(mesh):
    placed = (
        P(("grp", "sp"), None),
        P(("grp", "sp"), None),
        P(("grp", "sp"), None),
        P(("grp", "sp"), None),
        P(),
        P(),
        P(("grp", "sp")),
        P("grp"),
    )
    return jax.shard_map(
        body,
        mesh=mesh,
        in_specs=placed,
        out_specs=(
            P(("grp", "sp"), None),
            P(("grp", "sp"), None),
            P(("grp", "sp"), None),
            P(),
            P(),
        ),
        check_vma=False,
    )
```

profile of v0, /device:TPU:1, one launch (start us, length us, event | category | flops | bytes accessed | tf_op | source)
XLA Modules:
  0.0 534.9 jit_solution(859588045134463783)
XLA Ops:
  7.9 1.6 copy.109
  9.5 1.3 copy.110
  10.9 16.2 %all-to-all-start = ((bf16[128,16,256]{2,0,1:T(8,128)(2,1)}), bf16[128,16,256]{2,0,1:T(8,128)(2,1)S(1)}, u32[]{:S(2)}, u32[]{:S(2)}) async-start(bf16[128,16,256]{2,0,1:T(8,128)(2,1)} %copy.110), calls=%async_computation | async-start | bytes 2097152 | tf_op jit(solution)/shard_map/all_to_all | solution.py:116
  28.5 66.2 %all-gather = s32[16,1,128]{2,1,0:T(1,128)S(1)} all-gather(s32[1,1,128]{2,1,0:T(1,128)S(1)} %bitcast.397), channel_id=1, replica_groups=mesh['grp'=32,'sp'=16] {'sp'}, dimensions={0}, use_global_device_ids=true | all-gather | bytes 8704 | tf_op jit(solution)/shard_map/all_gather | solution.py:123
  98.3 1.3 copy.112
  100.8 12.3 %all-to-all-start.1 = ((bf16[128,16,256]{2,0,1:T(8,128)(2,1)}), bf16[128,16,256]{2,0,1:T(8,128)(2,1)S(1)}, u32[]{:S(2)}, u32[]{:S(2)}) async-start(bf16[128,16,256]{2,0,1:T(8,128)(2,1)} %copy.112), calls=%async_computation.1 | async-start | bytes 2097152 | tf_op jit(solution)/shard_map/all_to_all | solution.py:117
  116.6 18.2 %all-to-all-done.1 = bf16[128,16,256]{2,0,1:T(8,128)(2,1)S(1)} async-done(((bf16[128,16,256]{2,0,1:T(8,128)(2,1)}), bf16[128,16,256]{2,0,1:T(8,128)(2,1)S(1)}, u32[]{:S(2)}, u32[]{:S(2)}) %all-to-all-start.1) | async-done | bytes 1048608 | tf_op jit(solution)/shard_map/all_to_all | solution.py:117
  135.8 1.4 fusion.46
  137.3 1.4 fusion.48
  138.9 1.3 fusion.145
  140.2 95.2 %all-gather.6.cloned.1.call-done = bf16[2048,512]{1,0:T(8,128)(2,1)} async-done(((bf16[128,512]{1,0:T(8,128)(2,1)}), bf16[2048,512]{1,0:T(8,128)(2,1)}) %all-gather.6.cloned.1.call-update) | async-done | bytes 2097168 | tf_op jit(solution)/shard_map/all_gather | solution.py:122
  235.4 2.1 constant_dynamic-slice_fusion
  237.6 1.3 multiply_reduce_fusion
  240.5 2.1 fusion.146
  242.6 1.4 multiply_reduce_fusion.1
  245.6 1.9 fusion.147
  247.6 1.3 multiply_reduce_fusion.2
  252.2 2.2 fusion.148
  254.4 1.3 multiply_reduce_fusion.3
  257.4 1.2 fusion.56
  259.8 2.1 fusion.149
  262.5 1.6 multiply_reduce_fusion.4
  266.4 2.4 fusion.150
  268.8 1.6 multiply_reduce_fusion.5
  272.1 3.2 fusion.67
  275.3 3.2 fusion.69
  278.5 3.2 fusion.71
  281.6 3.2 fusion.73
  284.8 3.2 fusion.75
  288.0 3.2 fusion.77
  291.2 1.8 fusion.151
  293.1 1.6 multiply_reduce_fusion.6
  295.9 2.1 fusion.152
  298.0 1.6 multiply_reduce_fusion.7
  300.9 1.2 fusion.52
  302.1 2.9 fusion.45
  306.1 3.9 all-to-all-start.2
  315.4 2.2 fusion.79
  319.8 1.2 fusion.61
  321.1 19.1 %all-to-all-done.2 = bf16[16,128,256]{2,1,0:T(8,128)(2,1)S(1)} async-done(((bf16[16,128,256]{2,1,0:T(8,128)(2,1)}), bf16[16,128,256]{2,1,0:T(8,128)(2,1)S(1)}, u32[]{:S(2)}, u32[]{:S(2)}) %all-to-all-start.2) | async-done | bytes 1048608 | tf_op jit(solution)/shard_map/all_to_all | solution.py:180
  340.2 10.4 %all-to-all-start.3 = ((f32[16,128,128]{2,1,0:T(8,128)}), f32[16,128,128]{2,1,0:T(8,128)S(1)}, u32[]{:S(2)}, u32[]{:S(2)}) async-start(f32[16,128,128]{2,1,0:T(8,128)} %bitcast.92), calls=%async_computation.3 | async-start | bytes 2097152 | tf_op jit(solution)/shard_map/all_to_all | solution.py:182
  350.6 3.1 fusion.81
  357.5 27.1 %all-to-all-done.3 = f32[16,128,128]{2,1,0:T(8,128)S(1)} async-done(((f32[16,128,128]{2,1,0:T(8,128)}), f32[16,128,128]{2,1,0:T(8,128)S(1)}, u32[]{:S(2)}, u32[]{:S(2)}) %all-to-all-start.3) | async-done | bytes 1048608 | tf_op jit(solution)/shard_map/all_to_all | solution.py:182
  384.5 11.4 %all-to-all-start.4 = ((f32[16,128,128]{2,1,0:T(8,128)}), f32[16,128,128]{2,1,0:T(8,128)S(1)}, u32[]{:S(2)}, u32[]{:S(2)}) async-start(f32[16,128,128]{2,1,0:T(8,128)} %bitcast.113), calls=%async_computation.4 | async-start | bytes 2097152 | tf_op jit(solution)/shard_map/all_to_all | solution.py:183
  397.4 1.3 copy.124
  398.7 2.3 copy.145
  402.4 24.9 %all-to-all-done.4 = f32[16,128,128]{2,1,0:T(8,128)S(1)} async-done(((f32[16,128,128]{2,1,0:T(8,128)}), f32[16,128,128]{2,1,0:T(8,128)S(1)}, u32[]{:S(2)}, u32[]{:S(2)}) %all-to-all-start.4) | async-done | bytes 1048608 | tf_op jit(solution)/shard_map/all_to_all | solution.py:183
  428.2 98.8 %all-reduce.7 = (f32[128]{0:T(128)S(1)}, f32[128]{0:T(128)S(1)}) all-reduce(f32[128]{0:T(128)S(1)} %copy-done.111, f32[128]{0:T(128)S(1)} %bitcast_reduce_fusion.2), channel_id=1, replica_groups=mesh['grp'=32,'sp'=16] {'grp','sp'}, use_global_device_ids=true, to_apply=%region_35.36 | all-reduce | flops 256 | bytes 2048 | tf_op jit(solution)/shard_map/psum | solution.py:197
  (323 shorter events, 44.0 us)
Async XLA Ops:
  7.2 128.7 %all-gather.4.cloned.1.call-start = ((), (), s32[]{:S(2)}) async-start(), calls=%async_computation.5 | async-start | bytes 2228224 | tf_op jit(solution)/shard_map/all_gather | solution.py:121
  9.5 18.9 %copy-start.110 = (s32[128]{0:T(128)S(1)}, s32[128]{0:T(128)}, u32[]{:S(2)}) copy-start(s32[128]{0:T(128)} %param.14) | copy-start | bytes 1540
  9.5 88.1 %copy-start.25 = (bf16[128,4096]{1,0:T(8,128)(2,1)S(1)}, bf16[128,4096]{1,0:T(8,128)(2,1)}, u32[]{:S(2)}) copy-start(bf16[128,4096]{1,0:T(8,128)(2,1)} %param.11) | copy-start | bytes 3145732
  10.9 90.0 %all-to-all-start = ((bf16[128,16,256]{2,0,1:T(8,128)(2,1)}), bf16[128,16,256]{2,0,1:T(8,128)(2,1)S(1)}, u32[]{:S(2)}, u32[]{:S(2)}) async-start(bf16[128,16,256]{2,0,1:T(8,128)(2,1)} %copy.110), calls=%async_computation | async-start | bytes 2097152 | tf_op jit(solution)/shard_map/all_to_all | solution.py:116
  27.1 208.4 %all-gather.6.cloned.1.call-start = ((), (), s32[]{:S(2)}) async-start(), calls=%async_computation.6 | async-start | bytes 2228224 | tf_op jit(solution)/shard_map/all_gather | solution.py:122
  97.6 158.2 %copy-start.70 = (f32[4,128]{1,0:T(4,128)}, f32[4,128]{1,0:T(4,128)S(1)}, u32[]{:S(2)}) copy-start(f32[4,128]{1,0:T(4,128)S(1)} %get-tuple-element.128) | copy-start | bytes 6148
  97.6 16.9 %copy-start.84 = (s32[4,1,128]{2,1,0:T(1,128)}, s32[4,1,128]{2,1,0:T(1,128)S(1)}, u32[]{:S(2)}) copy-start(s32[4,1,128]{2,1,0:T(1,128)S(1)} %get-tuple-element.89) | copy-start | bytes 6148
  98.3 17.3 %copy-start.80 = (f32[128]{0:T(128)S(1)}, f32[128]{0:T(128)}, u32[]{:S(2)}) copy-start(f32[128]{0:T(128)} %param.12) | copy-start | bytes 1540
  100.2 148.6 %copy-start.73 = (f32[4,128]{1,0:T(4,128)}, f32[4,128]{1,0:T(4,128)S(1)}, u32[]{:S(2)}) copy-start(f32[4,128]{1,0:T(4,128)S(1)} %get-tuple-element.131) | copy-start | bytes 6148
  100.2 16.4 %copy-start.87 = (s32[4,128]{1,0:T(4,128)}, s32[4,128]{1,0:T(4,128)S(1)}, u32[]{:S(2)}) copy-start(s32[4,128]{1,0:T(4,128)S(1)} %get-tuple-element.93) | copy-start | bytes 6148
  100.2 16.4 %copy-start.89 = (s32[4,128]{1,0:T(4,128)}, s32[4,128]{1,0:T(4,128)S(1)}, u32[]{:S(2)}) copy-start(s32[4,128]{1,0:T(4,128)S(1)} %get-tuple-element.95) | copy-start | bytes 6148
  100.2 38.6 %copy-start.83 = (s32[4,128]{1,0:T(4,128)}, s32[4,128]{1,0:T(4,128)S(1)}, u32[]{:S(2)}) copy-start(s32[4,128]{1,0:T(4,128)S(1)} %get-tuple-element.94) | copy-start | bytes 6148
  100.8 34.0 %all-to-all-start.1 = ((bf16[128,16,256]{2,0,1:T(8,128)(2,1)}), bf16[128,16,256]{2,0,1:T(8,128)(2,1)S(1)}, u32[]{:S(2)}, u32[]{:S(2)}) async-start(bf16[128,16,256]{2,0,1:T(8,128)(2,1)} %copy.112), calls=%async_computation.1 | async-start | bytes 2097152 | tf_op jit(solution)/shard_map/all_to_all | solution.py:117
  114.5 24.3 %copy-start.94 = (s32[4,256]{1,0:T(4,128)}, s32[4,256]{1,0:T(4,128)S(1)}, u32[]{:S(2)}) copy-start(s32[4,256]{1,0:T(4,128)S(1)} %get-tuple-element.134) | copy-start | bytes 12292
  114.5 24.4 %copy-start.95 = (s32[4,256]{1,0:T(4,128)}, s32[4,256]{1,0:T(4,128)S(1)}, u32[]{:S(2)}) copy-start(s32[4,256]{1,0:T(4,128)S(1)} %get-tuple-element.135) | copy-start | bytes 12292
  115.9 21.3 %copy-start.90 = (f32[128]{0:T(128)S(1)}, f32[128]{0:T(128)}, u32[]{:S(2)}) copy-start(f32[128]{0:T(128)} %param.13) | copy-start | bytes 1540
  116.6 122.8 %copy-start.55 = (bf16[512,128]{1,0:T(8,128)(2,1)}, bf16[512,128]{1,0:T(8,128)(2,1)S(1)}, u32[]{:S(2)}) copy-start(bf16[512,128]{1,0:T(8,128)(2,1)S(1)} %get-tuple-element.84) | copy-start | bytes 393220
  116.6 123.9 %copy-start.53 = (bf16[512,128]{1,0:T(8,128)(2,1)}, bf16[512,128]{1,0:T(8,128)(2,1)S(1)}, u32[]{:S(2)}) copy-start(bf16[512,128]{1,0:T(8,128)(2,1)S(1)} %get-tuple-element.85) | copy-start | bytes 393220
  116.6 135.6 %copy-start.50 = (bf16[512,128]{1,0:T(8,128)(2,1)}, bf16[512,128]{1,0:T(8,128)(2,1)S(1)}, u32[]{:S(2)}) copy-start(bf16[512,128]{1,0:T(8,128)(2,1)S(1)} %get-tuple-element.83) | copy-start | bytes 393220
  138.8 110.3 %copy-start.13 = (bf16[512,128]{1,0:T(8,128)(2,1)}, bf16[512,128]{1,0:T(8,128)(2,1)S(1)}, u32[]{:S(2)}) copy-start(bf16[512,128]{1,0:T(8,128)(2,1)S(1)} %get-tuple-element.81) | copy-start | bytes 393220
  138.8 121.0 %copy-start.21 = (bf16[512,128]{1,0:T(8,128)(2,1)}, bf16[512,128]{1,0:T(8,128)(2,1)S(1)}, u32[]{:S(2)}) copy-start(bf16[512,128]{1,0:T(8,128)(2,1)S(1)} %get-tuple-element.76) | copy-start | bytes 393220
  138.8 121.0 %copy-start.23 = (bf16[512,128]{1,0:T(8,128)(2,1)}, bf16[512,128]{1,0:T(8,128)(2,1)S(1)}, u32[]{:S(2)}) copy-start(bf16[512,128]{1,0:T(8,128)(2,1)S(1)} %get-tuple-element.77) | copy-start | bytes 393220
  138.8 127.5 %copy-start.17 = (bf16[512,128]{1,0:T(8,128)(2,1)}, bf16[512,128]{1,0:T(8,128)(2,1)S(1)}, u32[]{:S(2)}) copy-start(bf16[512,128]{1,0:T(8,128)(2,1)S(1)} %get-tuple-element.78) | copy-start | bytes 393220
  138.8 127.5 %copy-start.19 = (bf16[512,128]{1,0:T(8,128)(2,1)}, bf16[512,128]{1,0:T(8,128)(2,1)S(1)}, u32[]{:S(2)}) copy-start(bf16[512,128]{1,0:T(8,128)(2,1)S(1)} %get-tuple-element.79) | copy-start | bytes 393220
  138.8 142.8 %copy-start.6 = (bf16[512,128]{1,0:T(8,128)(2,1)}, bf16[512,128]{1,0:T(8,128)(2,1)S(1)}, u32[]{:S(2)}) copy-start(bf16[512,128]{1,0:T(8,128)(2,1)S(1)} %get-tuple-element.82) | copy-start | bytes 393220
  138.9 152.4 %copy-start.10 = (bf16[512,128]{1,0:T(8,128)(2,1)}, bf16[512,128]{1,0:T(8,128)(2,1)S(1)}, u32[]{:S(2)}) copy-start(bf16[512,128]{1,0:T(8,128)(2,1)S(1)} %get-tuple-element.80) | copy-start | bytes 393220
  249.4 5.0 copy-start.64
  288.0 5.1 copy-start.62
  305.0 5.0 copy-start
  306.1 4.8 copy-start.1
  306.1 5.7 %copy-start.2 = (f32[4,256,128]{2,1,0:T(8,128)S(1)}, f32[4,256,128]{2,1,0:T(8,128)}, u32[]{:S(2)}) copy-start(f32[4,256,128]{2,1,0:T(8,128)} %convolution_multiply_fusion.2) | copy-start | bytes 1572868
  306.1 34.1 %all-to-all-start.2 = ((bf16[16,128,256]{2,1,0:T(8,128)(2,1)}), bf16[16,128,256]{2,1,0:T(8,128)(2,1)S(1)}, u32[]{:S(2)}, u32[]{:S(2)}) async-start(bf16[16,128,256]{2,1,0:T(8,128)(2,1)} %bitcast.70), calls=%async_computation.2 | async-start | bytes 2097152 | tf_op jit(solution)/shard_map/all_to_all | solution.py:180
  310.0 3.5 copy-start.4
  311.8 3.5 copy-start.57
  311.8 3.5 copy-start.63
  311.8 3.5 copy-start.75
  321.1 29.5 %copy-start.9 = (bf16[512,128]{1,0:T(8,128)(2,1)S(1)}, bf16[512,128]{1,0:T(8,128)(2,1)}, u32[]{:S(2)}) copy-start(bf16[512,128]{1,0:T(8,128)(2,1)} %copy-done.6) | copy-start | bytes 393220
  321.1 29.5 %copy-start.61 = (bf16[512,128]{1,0:T(8,128)(2,1)S(1)}, bf16[512,128]{1,0:T(8,128)(2,1)}, u32[]{:S(2)}) copy-start(bf16[512,128]{1,0:T(8,128)(2,1)} %get-tuple-element.31) | copy-start | bytes 393220
  321.1 29.5 %copy-start.72 = (f32[4,128]{1,0:T(4,128)S(1)}, f32[4,128]{1,0:T(4,128)}, u32[]{:S(2)}) copy-start(f32[4,128]{1,0:T(4,128)} %copy-done.70) | copy-start | bytes 6148
  321.1 29.5 %copy-start.86 = (s32[4,1,128]{2,1,0:T(1,128)S(1)}, s32[4,1,128]{2,1,0:T(1,128)}, u32[]{:S(2)}) copy-start(s32[4,1,128]{2,1,0:T(1,128)} %copy-done.84) | copy-start | bytes 6148
  321.1 29.5 %copy-start.92 = (s32[4,256]{1,0:T(4,128)S(1)}, s32[4,256]{1,0:T(4,128)}, u32[]{:S(2)}) copy-start(s32[4,256]{1,0:T(4,128)} %get-tuple-element.136) | copy-start | bytes 12292
  321.1 29.5 %copy-start.93 = (s32[4,256]{1,0:T(4,128)S(1)}, s32[4,256]{1,0:T(4,128)}, u32[]{:S(2)}) copy-start(s32[4,256]{1,0:T(4,128)} %get-tuple-element.137) | copy-start | bytes 12292
  340.2 44.4 %all-to-all-start.3 = ((f32[16,128,128]{2,1,0:T(8,128)}), f32[16,128,128]{2,1,0:T(8,128)S(1)}, u32[]{:S(2)}, u32[]{:S(2)}) async-start(f32[16,128,128]{2,1,0:T(8,128)} %bitcast.92), calls=%async_computation.3 | async-start | bytes 2097152 | tf_op jit(solution)/shard_map/all_to_all | solution.py:182
  357.4 38.5 %copy-start.48 = (bf16[128,512]{1,0:T(8,128)(2,1)S(1)}, bf16[128,512]{1,0:T(8,128)(2,1)}, u32[]{:S(2)}) copy-start(bf16[128,512]{1,0:T(8,128)(2,1)} %param.9) | copy-start | bytes 393220
  357.4 38.8 %copy-start.91 = (f32[128]{0:T(128)S(1)}, f32[128]{0:T(128)}, u32[]{:S(2)}) copy-start(f32[128]{0:T(128)} %param.13) | copy-start | bytes 1540
  357.5 38.8 %copy-start.109 = (f32[128]{0:T(128)S(1)}, f32[128]{0:T(128)}, u32[]{:S(2)}) copy-start(f32[128]{0:T(128)} %get-tuple-element.17) | copy-start | bytes 1540
  384.5 42.7 %all-to-all-start.4 = ((f32[16,128,128]{2,1,0:T(8,128)}), f32[16,128,128]{2,1,0:T(8,128)S(1)}, u32[]{:S(2)}, u32[]{:S(2)}) async-start(f32[16,128,128]{2,1,0:T(8,128)} %bitcast.113), calls=%async_computation.4 | async-start | bytes 2097152 | tf_op jit(solution)/shard_map/all_to_all | solution.py:183
  401.1 27.2 %copy-start.111 = (f32[128]{0:T(128)S(1)}, f32[128]{0:T(128)}, u32[]{:S(2)}) copy-start(f32[128]{0:T(128)} %add.309) | copy-start | bytes 1540
  (71 other events, 156.3 us)
Sparse Core Ops, SparseCore 0:
  11.2 118.3 all-gather.3
  132.8 102.5 all-gather.5
where the time goes:
time: 536 us; the launch traced here: 535 us
  waiting for transfers between devices  186 us (35%)
  blocking collectives  165 us (31%)
  matrix products  60.8 us (11%)
  starting transfers between devices  54.2 us (10%)
  local copies, waits for them, and re-layouts  27.2 us (5%)
  other arithmetic  25.8 us (5%)
  between operations  16.2 us (3%)
    psum x1, blocking collectives, body(): gain_totals = lax.psum((gain_q_part, gain_k_part), ('grp', 'sp'))  98.8 us
    all_gather x1, waiting for transfers between devices, body(): lax.all_gather(values, 'sp', axis=0, tiled=True)  95.2 us
    all_gather x1, blocking collectives, body(): lax.all_gather(doc_ids, 'sp', axis=0, tiled=True)  66.2 us
    all_to_all x1, waiting for transfers between devices, body(): lax.all_to_all(key_grad, 'sp', split_axis=0, concat_axis=1, tiled=True)  27.1 us
    all_to_all x1, waiting for transfers between devices, body(): lax.all_to_all(value_grad, 'sp', split_axis=0, concat_axis=1, tiled=True)  24.9 us
    dot_general x8, matrix products, block_grads(): jnp.einsum('nqk,nqd->nkd', attention_low, grad_part, preferred_element_ty...  24.3 us
    all_to_all x1, waiting for transfers between devices, body(): lax.all_to_all(grad_local, 'sp', split_axis=0, concat_axis=1, tiled=True)  19.1 us
    all_to_all x1, waiting for transfers between devices, body(): lax.all_to_all(grad_out, 'sp', split_axis=1, concat_axis=0, tiled=True)  18.2 us
  transfers between devices with their start and end apart: 7, of which 5 were waited for; matrix products, arithmetic and copies ran while one was open for 7% of the time, Pallas kernels for 0%

commit v1 on v0

v1 whole, which is shorter than its diff:
```python
import functools
import itertools
import math

import jax
import jax.numpy as jnp
from jax import lax
from jax.experimental import pallas as pl
from jax.experimental.pallas import tpu as pltpu
from jax.sharding import PartitionSpec as P

MESH = pl.DeviceIdType.MESH
F32 = jnp.float32
BF16 = jnp.bfloat16
eps = 1e-06
masked_score = -1e30
T = 128
HEADS = 32
KV = 4
GROUP = HEADS // KV
SPAN = dict(dx=4, dy=8, dz=8, dc=2)


def shifted(dx=0, dy=0, dz=0, dc=0):
    g, s = lax.axis_index("grp"), lax.axis_index("sp")
    x, y = g // 8, s // 2
    z, c = (s % 2) * 4 + (g // 2) % 4, g % 2
    x, y, z, c = (x + dx) % 4, (y + dy) % 8, (z + dz) % 8, (c + dc) % 2
    return (x * 8 + (z % 4) * 2 + c, y * 2 + z // 4)


def partners(axes):
    found = [
        dict(zip(axes, combo))
        for combo in itertools.product(*[range(SPAN[a]) for a in axes])
        if any(combo)
    ]

    def distance(d):
        return sum(min(v, SPAN[a] - v) for a, v in d.items() if a != "dc")

    return sorted(found, key=lambda d: -distance(d))


STAGES = (partners(("dc", "dz")), partners(("dx", "dy")))
PEERS = sum(len(s) for s in STAGES)


def contract(a, b, dims):
    return lax.dot_general(a, b, (dims, ((), ())), preferred_element_type=F32)


def kernel(
    q_hbm, k_hbm, v_hbm, g_hbm, gain_q_hbm, gain_k_hbm, doc_hbm, len_hbm,
    gq_out, gk_out, gv_out, gain_q_out, gain_k_out,
    q_in, g_in, k_in, v_in, gains, doc, length,
    k_halo, v_halo, doc_halo,
    qn, xhat, rfac, kn, kxhat, krfac, bias, live,
    dq, dk_own, dv_own, k_send, v_send, k_back, v_back, gq_stage,
    ar_send, ar_recv,
    in_sem, fwd_send, fwd_recv, ret_send, ret_recv, ars_sem, arr_sem, out_sem,
):
    sp = lax.axis_index("sp")
    grp = lax.axis_index("grp")
    has_prev, has_next = sp > 0, sp < 15
    early = sp % 2 == 0
    nxt, prv = (grp, (sp + 1) % 16), (grp, (sp + 15) % 16)
    scale = 1.0 / math.sqrt(T)

    barrier = pltpu.get_barrier_semaphore()

    def greet(d):
        pl.semaphore_signal(barrier, inc=1, device_id=d, device_id_type=MESH)

    @pl.when(has_next)
    def _():
        greet(nxt)

    @pl.when(has_prev)
    def _():
        greet(prv)

    for stage in STAGES:
        for d in stage:
            greet(shifted(**d))

    loads = [
        (k_hbm, k_in), (v_hbm, v_in), (doc_hbm, doc), (len_hbm, length),
        (gain_q_hbm, gains.at[pl.ds(0, 1)]), (gain_k_hbm, gains.at[pl.ds(1, 1)]),
    ]
    wide = GROUP * T
    for c in range(KV):
        cols = pl.ds(c * wide, wide)
        loads.append((q_hbm.at[:, cols], q_in.at[:, cols]))
        loads.append((g_hbm.at[:, cols], g_in.at[:, cols]))
    loads = [pltpu.make_async_copy(s, d, in_sem.at[i]) for i, (s, d) in enumerate(loads)]
    for cp in loads:
        cp.start()

    def forward(c):
        cols = pl.ds(c * T, T)
        return (
            pltpu.make_async_remote_copy(
                k_hbm.at[:, cols], k_halo.at[:, cols], fwd_send.at[2 * c], fwd_recv.at[2 * c],
                device_id=nxt, device_id_type=MESH,
            ),
            pltpu.make_async_remote_copy(
                v_hbm.at[:, cols], v_halo.at[:, cols], fwd_send.at[2 * c + 1],
                fwd_recv.at[2 * c + 1], device_id=nxt, device_id_type=MESH,
            ),
        )

    def doc_copy():
        return pltpu.make_async_remote_copy(
            doc_hbm, doc_halo, fwd_send.at[2 * KV], fwd_recv.at[2 * KV],
            device_id=nxt, device_id_type=MESH,
        )

    def open_and_send():
        near = has_next.astype(jnp.int32) + has_prev.astype(jnp.int32)
        pl.semaphore_wait(barrier, PEERS + near)

        @pl.when(has_next)
        def _():
            doc_copy().start()
            for c in range(KV):
                for cp in forward(c):
                    cp.start()

    @pl.when(jnp.logical_not(early))
    def _():
        open_and_send()

    for cp in loads[:6]:
        cp.wait()
    gain_q, gain_k = gains[0:1, :], gains[1:2, :]

    def factor(x):
        return lax.rsqrt(jnp.mean(x * x, axis=-1, keepdims=True) + eps)

    def norm_keys(raw, c, row):
        x = raw[:, c * T : (c + 1) * T].astype(F32)
        r = factor(x)
        xr = x * r
        kn[c, row : row + T, :] = (xr * gain_k).astype(BF16)
        kxhat[c, row : row + T, :] = xr
        return r

    for c in range(KV):
        krfac[c] = jnp.broadcast_to(norm_keys(k_in, c, T), (T, T))
    at_t = lax.broadcasted_iota(jnp.int32, (T, T), 1)
    at_s = lax.broadcasted_iota(jnp.int32, (T, T), 0)
    doc_t = jnp.broadcast_to(doc[...].astype(F32), (T, T))
    own = (doc_t == doc_t.T) & (at_s <= at_t)
    bias[T:, :] = jnp.where(own, 0.0, masked_score)
    place = sp * T + lax.broadcasted_iota(jnp.int32, (1, T), 1)
    live[...] = jnp.where(place < length[0], 1.0, 0.0)

    for c in range(KV):
        loads[6 + 2 * c].wait()
        loads[7 + 2 * c].wait()

        def norm_query(i, carry, c=c):
            h = c * GROUP + i
            cols = pl.ds(pl.multiple_of(h * T, T), T)
            x = q_in[:, cols].astype(F32)
            r = factor(x)
            xr = x * r
            qn[h] = (xr * gain_q).astype(BF16)
            xhat[h] = xr
            rfac[h] = jnp.broadcast_to(r, (T, T))
            return carry

        lax.fori_loop(0, GROUP, norm_query, 0, unroll=4)

    @pl.when(early)
    def _():
        open_and_send()

    @pl.when(has_prev)
    def _():
        doc_copy().wait_recv()

    @pl.when(jnp.logical_not(has_prev))
    def _():
        doc_halo[...] = jnp.zeros_like(doc_halo)
        k_halo[...] = jnp.zeros_like(k_halo)
        v_halo[...] = jnp.zeros_like(v_halo)

    doc_s = jnp.broadcast_to(doc_halo[...].astype(F32), (T, T)).T
    first = jnp.where(has_prev, 0.0, masked_score)
    bias[:T, :] = jnp.where(doc_s == doc_t, first, masked_score)

    def back(c):
        cols = pl.ds(c * T, T)
        return (
            pltpu.make_async_remote_copy(
                k_send.at[:, cols], k_back.at[:, cols], ret_send.at[2 * c], ret_recv.at[2 * c],
                device_id=prv, device_id_type=MESH,
            ),
            pltpu.make_async_remote_copy(
                v_send.at[:, cols], v_back.at[:, cols], ret_send.at[2 * c + 1],
                ret_recv.at[2 * c + 1], device_id=prv, device_id_type=MESH,
            ),
        )

    gain_q_sum = jnp.zeros((T, T), F32)
    gain_k_sum = jnp.zeros((2 * T, T), F32)
    for c in range(KV):
        cols = slice(c * T, (c + 1) * T)

        @pl.when(has_prev)
        def _(c=c):
            for cp in forward(c):
                cp.wait_recv()

        norm_keys(k_halo, c, 0)
        key = kn[c]
        value = jnp.concatenate([v_halo[:, cols], v_in[:, cols]], axis=0)

        def pair(i, carry, c=c, key=key, value=value):
            dk, dv, gq_sum = carry
            h = c * GROUP + 2 * i
            query = jnp.concatenate([qn[h], qn[h + 1]], axis=0)
            col0 = pl.ds(pl.multiple_of(h * T, T), T)
            col1 = pl.ds(pl.multiple_of(h * T + T, T), T)
            grad = jnp.concatenate([g_in[:, col0], g_in[:, col1]], axis=0)
            both = jnp.concatenate([bias[...], bias[...]], axis=1)
            score = contract(key, query, ((1,), (1,))) + both
            high = jnp.max(score, axis=0, keepdims=True)
            weight = jnp.exp((score - high) * scale)
            total = jnp.sum(weight, axis=0, keepdims=True)
            alive = jnp.concatenate([live[...], live[...]], axis=1)
            att = weight * (alive / total)
            gatt = contract(value, grad, ((1,), (1,)))
            delta = jnp.sum(att * gatt, axis=0, keepdims=True)
            ds = (att * (gatt - delta)).astype(BF16)
            dk = dk + contract(ds, query, ((1,), (0,)))
            dv = dv + contract(att.astype(BF16), grad, ((1,), (0,)))
            dq2 = contract(ds, key, ((0,), (0,))) * scale
            dq[h] = dq2[:T]
            dq[h + 1] = dq2[T:]
            gq_sum = gq_sum + dq2[:T] * xhat[h] + dq2[T:] * xhat[h + 1]
            return dk, dv, gq_sum

        zero = jnp.zeros((2 * T, T), F32)
        dk, dv, gain_q_sum = lax.fori_loop(0, GROUP // 2, pair, (zero, zero, gain_q_sum), unroll=2)
        dk = dk * scale
        gain_k_sum = gain_k_sum + dk * kxhat[c]
        dk_own[:, cols] = dk[T:]
        dv_own[:, cols] = dv[T:]
        k_send[:, cols] = dk[:T].astype(BF16)
        v_send[:, cols] = dv[:T].astype(BF16)

        @pl.when(has_prev)
        def _(c=c):
            for cp in back(c):
                cp.start()

    sums = jnp.concatenate(
        [
            jnp.sum(gain_q_sum, axis=0, keepdims=True),
            jnp.sum(gain_k_sum, axis=0, keepdims=True),
            jnp.zeros((6, T), F32),
        ],
        axis=0,
    )

    def exchange(stage):
        base = sum(len(s) for s in STAGES[:stage])
        return [
            pltpu.make_async_remote_copy(
                ar_send.at[stage], ar_recv.at[base + i], ars_sem.at[base + i],
                arr_sem.at[base + i], device_id=shifted(**d), device_id_type=MESH,
            )
            for i, d in enumerate(STAGES[stage])
        ]

    def gather_sums(stage, sums):
        base = sum(len(s) for s in STAGES[:stage])
        for i, cp in enumerate(exchange(stage)):
            cp.wait_recv()
            sums = sums + ar_recv[base + i]
        return sums

    ar_send[0] = sums
    for cp in exchange(0):
        cp.start()

    def backward(xr, r, gain, up):
        u = gain * up
        return r * (u - xr * jnp.mean(u * xr, axis=-1, keepdims=True))

    writes = []
    for c in range(KV):

        def query_grad(i, carry, c=c):
            h = c * GROUP + i
            cols = pl.ds(pl.multiple_of(h * T, T), T)
            gq_stage[:, cols] = backward(xhat[h], rfac[h], gain_q, dq[h]).astype(BF16)
            return carry

        lax.fori_loop(0, GROUP, query_grad, 0, unroll=4)
        cols = pl.ds(c * wide, wide)
        cp = pltpu.make_async_copy(gq_stage.at[:, cols], gq_out.at[:, cols], out_sem.at[c])
        cp.start()
        writes.append(cp)

    sums = gather_sums(0, sums)
    ar_send[1] = sums
    for cp in exchange(1):
        cp.start()

    for c in range(KV):
        cols = slice(c * T, (c + 1) * T)

        @pl.when(has_next)
        def _(c=c, cols=cols):
            for cp in back(c):
                cp.wait_recv()
            dk_own[:, cols] = dk_own[:, cols] + k_back[:, cols].astype(F32)
            dv_own[:, cols] = dv_own[:, cols] + v_back[:, cols].astype(F32)

        gk_out[:, cols] = backward(kxhat[c, T:, :], krfac[c], gain_k, dk_own[:, cols]).astype(BF16)
        gv_out[:, cols] = dv_own[:, cols].astype(BF16)

    sums = gather_sums(1, sums) * (1.0 / math.sqrt(T * 512))
    gain_q_out[...] = sums[0:1, :]
    gain_k_out[...] = sums[1:2, :]

    @pl.when(has_next)
    def _():
        doc_copy().wait_send()
        for c in range(KV):
            for cp in forward(c):
                cp.wait_send()

    @pl.when(has_prev)
    def _():
        for c in range(KV):
            for cp in back(c):
                cp.wait_send()

    for stage in range(len(STAGES)):
        for cp in exchange(stage):
            cp.wait_send()
    for cp in writes:
        cp.wait()


def body(queries, keys, values, grad_out, gain_q, gain_k, doc_ids, bucket_len):
    anywhere = pl.BlockSpec(memory_space=pl.ANY)
    vmem = pl.BlockSpec(memory_space=pltpu.VMEM)
    wide, narrow = queries.shape, keys.shape
    dma = pltpu.SemaphoreType.DMA
    outs = pl.pallas_call(
        kernel,
        out_shape=(
            jax.ShapeDtypeStruct(wide, BF16),
            jax.ShapeDtypeStruct(narrow, BF16),
            jax.ShapeDtypeStruct(narrow, BF16),
            jax.ShapeDtypeStruct((1, T), F32),
            jax.ShapeDtypeStruct((1, T), F32),
        ),
        in_specs=[anywhere] * 8,
        out_specs=(anywhere, vmem, vmem, vmem, vmem),
        scratch_shapes=[
            pltpu.VMEM(wide, BF16), pltpu.VMEM(wide, BF16),
            pltpu.VMEM(narrow, BF16), pltpu.VMEM(narrow, BF16),
            pltpu.VMEM((2, T), F32), pltpu.VMEM((1, T), jnp.int32), pltpu.SMEM((1,), jnp.int32),
            pltpu.VMEM(narrow, BF16), pltpu.VMEM(narrow, BF16), pltpu.VMEM((1, T), jnp.int32),
            pltpu.VMEM((HEADS, T, T), BF16), pltpu.VMEM((HEADS, T, T), F32),
            pltpu.VMEM((HEADS, T, T), F32),
            pltpu.VMEM((KV, 2 * T, T), BF16), pltpu.VMEM((KV, 2 * T, T), F32),
            pltpu.VMEM((KV, T, T), F32),
            pltpu.VMEM((2 * T, T), F32), pltpu.VMEM((1, T), F32),
            pltpu.VMEM((HEADS, T, T), F32),
            pltpu.VMEM(narrow, F32), pltpu.VMEM(narrow, F32),
            pltpu.VMEM(narrow, BF16), pltpu.VMEM(narrow, BF16),
            pltpu.VMEM(narrow, BF16), pltpu.VMEM(narrow, BF16),
            pltpu.VMEM(wide, BF16),
            pltpu.VMEM((2, 8, T), F32), pltpu.VMEM((PEERS, 8, T), F32),
            dma((14,)), dma((9,)), dma((9,)), dma((8,)), dma((8,)),
            dma((PEERS,)), dma((PEERS,)), dma((KV,)),
        ],
        compiler_params=pltpu.CompilerParams(
            collective_id=0, has_side_effects=True, vmem_limit_bytes=60 * 2**20
        ),
    )(
        queries, keys, values, grad_out, gain_q.reshape(1, T), gain_k.reshape(1, T),
        doc_ids.reshape(1, T), bucket_len,
    )
    return outs[0], outs[1], outs[2], outs[3].reshape(T), outs[4].reshape(T)


def solution(mesh):
    rows = P(("grp", "sp"), None)
    return jax.shard_map(
        body,
        mesh=mesh,
        in_specs=(rows, rows, rows, rows, P(), P(), P(("grp", "sp")), P("grp")),
        out_specs=(rows, rows, rows, P(), P()),
        check_vma=False,
    )
```

time: 536 us -> 65.7 us (0.12)
  waiting for transfers between devices: 186 us -> 0 us
  blocking collectives: 165 us -> 0 us
  matrix products: 60.8 us -> 0 us
  Pallas kernels: 0 us -> 59.2 us
  starting transfers between devices: 54.2 us -> 0 us
  other arithmetic: 25.8 us -> 0 us
  local copies, waits for them, and re-layouts: 27.2 us -> 5.03 us
  between operations: 16.2 us -> 1.3 us
    psum x1 -> x0, blocking collectives: 98.8 us -> none  [body(): gain_totals = lax.psum((gain_q_part, gain_k_part), ('grp', 'sp'))]
    all_gather x2 -> x0, waiting for transfers between devices: 95.2 us -> none  [the longest x1 95.2 us: body(): lax.all_gather(values, 'sp', axis=0, tiled=True)]
    all_to_all x5 -> x0, waiting for transfers between devices: 89.2 us -> none  [the longest x1 27.1 us: body(): lax.all_to_all(key_grad, 'sp', split_axis=0, concat_axis=1, tiled=True)]
    all_gather x1 -> x0, blocking collectives: 66.2 us -> none  [body(): lax.all_gather(doc_ids, 'sp', axis=0, tiled=True)]
    pallas_call x0 -> x1, Pallas kernels: none -> 59.2 us  [body(): pl.pallas_call(kernel, out_shape=(jax.ShapeDtypeStruct(wide, BF16), jax.S...]
    all_to_all x5 -> x0, starting transfers between devices: 54.1 us -> none  [the longest x1 16.2 us: body(): lax.all_to_all(queries, 'sp', split_axis=1, concat_axis=0, tiled=True)]
    dot_general x32 -> x0, matrix products: 44.9 us -> none  [the longest x8 24.3 us: block_grads(): jnp.einsum('nqk,nqd->nkd', attention_low, grad_part, preferred_element_ty...]
    sub x8 -> x0, matrix products: 15.9 us -> none  [block_grads(): weights = jnp.exp(scores - highest)]
  transfers between devices with their start and end apart: 7 -> 0, of which waited for: 5 -> 0; matrix products, arithmetic and copies ran while one was open for 7% -> 0% of each run, Pallas kernels for 0% -> 0%
where the time goes in v1:
time: 65.7 us; the launch traced here: 65.5 us
  Pallas kernels  59.2 us (90%)
  local copies, waits for them, and re-layouts  5.03 us (8%)
  between operations  1.3 us (2%)
    pallas_call x1, Pallas kernels, body(): pl.pallas_call(kernel, out_shape=(jax.ShapeDtypeStruct(wide, BF16), jax.S...  59.2 us
    unnamed x13, local copies, waits for them, and re-layouts  5.03 us

profile of v1, /device:TPU:1, one launch (start us, length us, event | category | flops | bytes accessed | tf_op | source)
XLA Modules:
  0.0 65.5 jit_solution(2797642204415247350)
XLA Ops:
  1.3 59.2 %shard_map.119 = (bf16[128,4096]{1,0:T(8,128)(2,1)}, bf16[128,512]{1,0:T(8,128)(2,1)}, bf16[128,512]{1,0:T(8,128)(2,1)}, f32[1,128]{1,0:T(1,128)}, f32[1,128]{1,0:T(1,128)}) custom-call(bf16[128,4096]{1,0:T(8,128)(2,1)} %q_hbm.1, bf16[128,512]{1,0:T(8,128)(2,1)} %k_hbm.1, bf16[128,512]{1,0:T(8,128)(2,1)} %v_hbm.1, bf16[128,4096]{1,0:T(8,128)(2,1)} %g_hbm.1, ...), custom_call_target="tpu_custom_call" | custom-call | tf_op jit(solution)/shard_map/pallas_call | solution.py:356
  60.4 0.0 copy-start.1
  60.5 2.3 %copy.19 = bf16[128,4096]{1,0:T(8,128)(2,1)} copy(bf16[128,4096]{1,0:T(8,128)(2,1)} %get-tuple-element.20) | data formatting | bytes 2097152
  62.8 0.0 copy-done.1
  62.8 0.0 copy-start
  62.8 0.7 %copy.20 = bf16[128,512]{1,0:T(8,128)(2,1)} copy(bf16[128,512]{1,0:T(8,128)(2,1)S(1)} %copy-done.1) | data formatting | bytes 262144
  63.4 0.3 copy-done
  63.7 0.0 copy-start.3
  63.7 0.7 copy.21
  64.4 0.0 copy-done.3
  64.4 0.0 copy-start.2
  64.4 0.5 copy.22
  64.9 0.1 copy-done.2
  65.0 0.5 copy.23
Async XLA Ops:
  60.4 2.3 %copy-start.1 = (bf16[128,512]{1,0:T(8,128)(2,1)S(1)}, bf16[128,512]{1,0:T(8,128)(2,1)}, u32[]{:S(2)}) copy-start(bf16[128,512]{1,0:T(8,128)(2,1)} %get-tuple-element.21) | copy-start | bytes 393220
  62.8 1.0 %copy-start = (bf16[128,512]{1,0:T(8,128)(2,1)S(1)}, bf16[128,512]{1,0:T(8,128)(2,1)}, u32[]{:S(2)}) copy-start(bf16[128,512]{1,0:T(8,128)(2,1)} %get-tuple-element.22) | copy-start | bytes 393220
  63.7 0.7 %copy-start.3 = (f32[1,128]{1,0:T(1,128)S(1)}, f32[1,128]{1,0:T(1,128)}, u32[]{:S(2)}) copy-start(f32[1,128]{1,0:T(1,128)} %get-tuple-element.13) | copy-start | bytes 1540
  64.4 0.6 copy-start.2

commit v2 on v1

--- a/solution.py
+++ b/solution.py
@@ -1,5 +1,4 @@
 import functools
-import itertools
 import math
 
 import jax
@@ -18,32 +17,31 @@
 HEADS = 32
 KV = 4
 GROUP = HEADS // KV
-SPAN = dict(dx=4, dy=8, dz=8, dc=2)
-
-
-def shifted(dx=0, dy=0, dz=0, dc=0):
+STAGES = 3
+SIDE = 8
+EARLY = 0
+PARTS = 4
+
+
+def ring(value, step, size):
+    return lax.rem(value + step, size)
+
+
+def places():
     g, s = lax.axis_index("grp"), lax.axis_index("sp")
-    x, y = g // 8, s // 2
-    z, c = (s % 2) * 4 + (g // 2) % 4, g % 2
-    x, y, z, c = (x + dx) % 4, (y + dy) % 8, (z + dz) % 8, (c + dc) % 2
-    return (x * 8 + (z % 4) * 2 + c, y * 2 + z // 4)
-
-
-def partners(axes):
-    found = [
-        dict(zip(axes, combo))
-        for combo in itertools.product(*[range(SPAN[a]) for a in axes])
-        if any(combo)
-    ]
-
-    def distance(d):
-        return sum(min(v, SPAN[a] - v) for a, v in d.items() if a != "dc")
-
-    return sorted(found, key=lambda d: -distance(d))
-
-
-STAGES = (partners(("dc", "dz")), partners(("dx", "dy")))
-PEERS = sum(len(s) for s in STAGES)
+    x, z_lo, c = lax.div(g, 8), lax.rem(lax.div(g, 2), 4), lax.rem(g, 2)
+    y, z_hi = lax.div(s, 2), lax.rem(s, 2)
+
+    def along_z(z):
+        return (x * 8 + lax.rem(z, 4) * 2 + c, y * 2 + lax.div(z, 4))
+
+    def along_y(at):
+        return (g, at * 2 + z_hi)
+
+    def along_xc(at):
+        return (lax.div(at, 2) * 8 + z_lo * 2 + lax.rem(at, 2), s)
+
+    return ((z_hi * 4 + z_lo, along_z), (y, along_y), (x * 2 + c, along_xc))
 
 
 def contract(a, b, dims):
@@ -52,7 +50,7 @@
 
 def kernel(
     q_hbm, k_hbm, v_hbm, g_hbm, gain_q_hbm, gain_k_hbm, doc_hbm, len_hbm,
-    gq_out, gk_out, gv_out, gain_q_out, gain_k_out,
+    gq_out, gk_out, gv_out, gain_out,
     q_in, g_in, k_in, v_in, gains, doc, length,
     k_halo, v_halo, doc_halo,
     qn, xhat, rfac, kn, kxhat, krfac, bias, live,
@@ -80,9 +78,10 @@
     def _():
         greet(prv)
 
-    for stage in STAGES:
-        for d in stage:
-            greet(shifted(**d))
+    rows = places()
+    for here, device in rows:
+        for step in (4, 3, 5, 2, 6, 1, 7):
+            greet(device(ring(here, step, SIDE)))
 
     loads = [
         (k_hbm, k_in), (v_hbm, v_in), (doc_hbm, doc), (len_hbm, length),
@@ -118,7 +117,7 @@
 
     def open_and_send():
         near = has_next.astype(jnp.int32) + has_prev.astype(jnp.int32)
-        pl.semaphore_wait(barrier, PEERS + near)
+        pl.semaphore_wait(barrier, STAGES * (SIDE - 1) + near)
 
         @pl.when(has_next)
         def _():
@@ -154,7 +153,7 @@
     own = (doc_t == doc_t.T) & (at_s <= at_t)
     bias[T:, :] = jnp.where(own, 0.0, masked_score)
     place = sp * T + lax.broadcasted_iota(jnp.int32, (1, T), 1)
-    live[...] = jnp.where(place < length[0], 1.0, 0.0)
+    live[...] = jnp.where(place < length[...], 1.0, 0.0)
 
     for c in range(KV):
         loads[6 + 2 * c].wait()
@@ -252,40 +251,57 @@
         k_send[:, cols] = dk[:T].astype(BF16)
         v_send[:, cols] = dv[:T].astype(BF16)
 
-        @pl.when(has_prev)
-        def _(c=c):
-            for cp in back(c):
-                cp.start()
+        if c < EARLY:
+
+            @pl.when(has_prev)
+            def _(c=c):
+                for cp in back(c):
+                    cp.start()
 
     sums = jnp.concatenate(
         [
             jnp.sum(gain_q_sum, axis=0, keepdims=True),
             jnp.sum(gain_k_sum, axis=0, keepdims=True),
-            jnp.zeros((6, T), F32),
         ],
         axis=0,
     )
 
     def exchange(stage):
-        base = sum(len(s) for s in STAGES[:stage])
+        here, device = rows[stage]
         return [
             pltpu.make_async_remote_copy(
-                ar_send.at[stage], ar_recv.at[base + i], ars_sem.at[base + i],
-                arr_sem.at[base + i], device_id=shifted(**d), device_id_type=MESH,
+                ar_send.at[stage], ar_recv.at[stage, here], ars_sem.at[stage, step - 1],
+                arr_sem.at[stage, here], device_id=device(ring(here, step, SIDE)),
+                device_id_type=MESH,
             )
-            for i, d in enumerate(STAGES[stage])
+            for step in (4, 3, 5, 2, 6, 1, 7)
         ]
 
-    def gather_sums(stage, sums):
-        base = sum(len(s) for s in STAGES[:stage])
-        for i, cp in enumerate(exchange(stage)):
-            cp.wait_recv()
-            sums = sums + ar_recv[base + i]
-        return sums
-
-    ar_send[0] = sums
-    for cp in exchange(0):
-        cp.start()
+    def send_sums(stage, sums):
+        ar_send[stage] = sums
+        ar_recv[stage, rows[stage][0]] = sums
+        for cp in exchange(stage):
+            cp.start()
+
+    def gather_sums(stage):
+        here, _ = rows[stage]
+        for step in range(1, SIDE):
+            at = ring(here, step, SIDE)
+            pltpu.make_async_copy(
+                ar_recv.at[stage, at], ar_recv.at[stage, at], arr_sem.at[stage, at]
+            ).wait()
+        total = ar_recv[stage, 0]
+        for at in range(1, SIDE):
+            total = total + ar_recv[stage, at]
+        return total
+
+    send_sums(0, sums)
+
+    @pl.when(has_prev)
+    def _():
+        for c in range(EARLY, KV):
+            for cp in back(c):
+                cp.start()
 
     def backward(xr, r, gain, up):
         u = gain * up
@@ -306,10 +322,9 @@
         cp.start()
         writes.append(cp)
 
-    sums = gather_sums(0, sums)
-    ar_send[1] = sums
-    for cp in exchange(1):
-        cp.start()
+    send_sums(1, gather_sums(0))
+
+    send_sums(2, gather_sums(1))
 
     for c in range(KV):
         cols = slice(c * T, (c + 1) * T)
@@ -324,9 +339,7 @@
         gk_out[:, cols] = backward(kxhat[c, T:, :], krfac[c], gain_k, dk_own[:, cols]).astype(BF16)
         gv_out[:, cols] = dv_own[:, cols].astype(BF16)
 
-    sums = gather_sums(1, sums) * (1.0 / math.sqrt(T * 512))
-    gain_q_out[...] = sums[0:1, :]
-    gain_k_out[...] = sums[1:2, :]
+    gain_out[...] = gather_sums(2) * (1.0 / math.sqrt(T * 512))
 
     @pl.when(has_next)
     def _():
@@ -341,15 +354,36 @@
             for cp in back(c):
                 cp.wait_send()
 
-    for stage in range(len(STAGES)):
+    for stage in range(STAGES):
         for cp in exchange(stage):
             cp.wait_send()
     for cp in writes:
         cp.wait()
 
 
+def hand_over(gq, gk, gv, gain, gq_out, gk_out, gv_out, gain_q_out, gain_k_out, wide, near, last, sem):
+    pairs = [(gk, near.at[0], gk_out), (gv, near.at[1], gv_out)]
+    pairs += [
+        (gain.at[pl.ds(i, 1)], last.at[pl.ds(i, 1)], out)
+        for i, out in enumerate((gain_q_out, gain_k_out))
+    ]
+    part = T // PARTS
+    for i in range(PARTS):
+        at = pl.ds(i * part, part)
+        pairs.append((gq.at[at], wide.at[at], gq_out.at[at]))
+    reads = [pltpu.make_async_copy(a, b, sem.at[0, i]) for i, (a, b, _) in enumerate(pairs)]
+    writes = [pltpu.make_async_copy(b, c, sem.at[1, i]) for i, (_, b, c) in enumerate(pairs)]
+    for cp in reads:
+        cp.start()
+    for read, write in zip(reads, writes):
+        read.wait()
+        write.start()
+    for cp in writes:
+        cp.wait()
+
+
 def body(queries, keys, values, grad_out, gain_q, gain_k, doc_ids, bucket_len):
-    anywhere = pl.BlockSpec(memory_space=pl.ANY)
+    hbm = pl.BlockSpec(memory_space=pltpu.HBM)
     vmem = pl.BlockSpec(memory_space=pltpu.VMEM)
     wide, narrow = queries.shape, keys.shape
     dma = pltpu.SemaphoreType.DMA
@@ -359,15 +393,14 @@
             jax.ShapeDtypeStruct(wide, BF16),
             jax.ShapeDtypeStruct(narrow, BF16),
             jax.ShapeDtypeStruct(narrow, BF16),
-            jax.ShapeDtypeStruct((1, T), F32),
-            jax.ShapeDtypeStruct((1, T), F32),
+            jax.ShapeDtypeStruct((2, T), F32),
         ),
-        in_specs=[anywhere] * 8,
-        out_specs=(anywhere, vmem, vmem, vmem, vmem),
+        in_specs=[hbm] * 8,
+        out_specs=(hbm, vmem, vmem, vmem),
         scratch_shapes=[
             pltpu.VMEM(wide, BF16), pltpu.VMEM(wide, BF16),
             pltpu.VMEM(narrow, BF16), pltpu.VMEM(narrow, BF16),
-            pltpu.VMEM((2, T), F32), pltpu.VMEM((1, T), jnp.int32), pltpu.SMEM((1,), jnp.int32),
+            pltpu.VMEM((2, T), F32), pltpu.VMEM((1, T), jnp.int32), pltpu.VMEM((1, 1), jnp.int32),
             pltpu.VMEM(narrow, BF16), pltpu.VMEM(narrow, BF16), pltpu.VMEM((1, T), jnp.int32),
             pltpu.VMEM((HEADS, T, T), BF16), pltpu.VMEM((HEADS, T, T), F32),
             pltpu.VMEM((HEADS, T, T), F32),
@@ -379,18 +412,35 @@
             pltpu.VMEM(narrow, BF16), pltpu.VMEM(narrow, BF16),
             pltpu.VMEM(narrow, BF16), pltpu.VMEM(narrow, BF16),
             pltpu.VMEM(wide, BF16),
-            pltpu.VMEM((2, 8, T), F32), pltpu.VMEM((PEERS, 8, T), F32),
+            pltpu.VMEM((STAGES, 2, T), F32), pltpu.VMEM((STAGES, SIDE, 2, T), F32),
             dma((14,)), dma((9,)), dma((9,)), dma((8,)), dma((8,)),
-            dma((PEERS,)), dma((PEERS,)), dma((KV,)),
+            dma((STAGES, SIDE - 1)), dma((STAGES, SIDE)), dma((KV,)),
         ],
         compiler_params=pltpu.CompilerParams(
             collective_id=0, has_side_effects=True, vmem_limit_bytes=60 * 2**20
         ),
     )(
         queries, keys, values, grad_out, gain_q.reshape(1, T), gain_k.reshape(1, T),
-        doc_ids.reshape(1, T), bucket_len,
+        doc_ids.reshape(1, T), bucket_len.reshape(1, 1),
     )
-    return outs[0], outs[1], outs[2], outs[3].reshape(T), outs[4].reshape(T)
+    done = pl.pallas_call(
+        hand_over,
+        out_shape=(
+            jax.ShapeDtypeStruct(wide, BF16),
+            jax.ShapeDtypeStruct(narrow, BF16),
+            jax.ShapeDtypeStruct(narrow, BF16),
+            jax.ShapeDtypeStruct((1, T), F32),
+            jax.ShapeDtypeStruct((1, T), F32),
+        ),
+        in_specs=[hbm] * 4,
+        out_specs=(hbm,) * 5,
+        scratch_shapes=[
+            pltpu.VMEM(wide, BF16), pltpu.VMEM((2,) + narrow, BF16), pltpu.VMEM((2, T), F32),
+            dma((2, PARTS + 4)),
+        ],
+        compiler_params=pltpu.CompilerParams(vmem_limit_bytes=60 * 2**20),
+    )(*outs)
+    return done[0], done[1], done[2], done[3].reshape(T), done[4].reshape(T)
 
 
 def solution(mesh):

time: 65.7 us -> 52.2 us (0.79)
  Pallas kernels: 59.2 us -> 50.8 us
  local copies, waits for them, and re-layouts: 5.03 us -> 0 us
    pallas_call x1, Pallas kernels: 59.2 us -> 48.6 us  [body(): pl.pallas_call(kernel, out_shape=(jax.ShapeDtypeStruct(wide, BF16), jax.S...]
    unnamed x13 -> x0, local copies, waits for them, and re-layouts: 5.03 us -> none
    pallas_call x0 -> x1, Pallas kernels: none -> 2.2 us  [body(): pl.pallas_call(hand_over, out_shape=(jax.ShapeDtypeStruct(wide, BF16), ja...]
where the time goes in v2:
time: 52.2 us; the launch traced here: 52 us
  Pallas kernels  50.8 us (97%)
  between operations  1.29 us (2%)
    pallas_call x1, Pallas kernels, body(): pl.pallas_call(kernel, out_shape=(jax.ShapeDtypeStruct(wide, BF16), jax.S...  48.6 us
    pallas_call x1, Pallas kernels, body(): pl.pallas_call(hand_over, out_shape=(jax.ShapeDtypeStruct(wide, BF16), ja...  2.2 us

profile of v2, /device:TPU:1, one launch (start us, length us, event | category | flops | bytes accessed | tf_op | source)
XLA Modules:
  0.0 52.0 jit_solution(13857473973559829708)
XLA Ops:
  1.3 48.6 %shard_map.119 = (bf16[128,4096]{1,0:T(8,128)(2,1)}, bf16[128,512]{1,0:T(8,128)(2,1)}, bf16[128,512]{1,0:T(8,128)(2,1)}, f32[2,128]{1,0:T(2,128)}) custom-call(bf16[128,4096]{1,0:T(8,128)(2,1)} %q_hbm.1, bf16[128,512]{1,0:T(8,128)(2,1)} %k_hbm.1, bf16[128,512]{1,0:T(8,128)(2,1)} %v_hbm.1, bf16[128,4096]{1,0:T(8,128)(2,1)} %g_hbm.1, f32[1,128]{1,0:T(1,128)} %bitcast.7, ...), custom_call_target="tpu_custom_call" | custom-call | tf_op jit(solution)/shard_map/pallas_call | solution.py:390
  49.8 2.2 %shard_map.120 = (bf16[128,4096]{1,0:T(8,128)(2,1)}, bf16[128,512]{1,0:T(8,128)(2,1)}, bf16[128,512]{1,0:T(8,128)(2,1)}, f32[1,128]{1,0:T(1,128)}, f32[1,128]{1,0:T(1,128)}) custom-call(bf16[128,4096]{1,0:T(8,128)(2,1)} %get-tuple-element.14.gq, bf16[128,512]{1,0:T(8,128)(2,1)} %get-tuple-element.15.gk, bf16[128,512]{1,0:T(8,128)(2,1)} %get-tuple-element.16.gv, ...), custom_call_target="tpu_custom_call" | custom-call | tf_op jit(solution)/shard_map/pallas_call | solution.py:426

commit v3 on v2

--- a/solution.py
+++ b/solution.py
@@ -17,31 +17,37 @@
 HEADS = 32
 KV = 4
 GROUP = HEADS // KV
-STAGES = 3
-SIDE = 8
-EARLY = 0
+SIDES = (8, 8, 8)
 PARTS = 4
 
 
 def ring(value, step, size):
-    return lax.rem(value + step, size)
+    moved = value + step
+    return jnp.where(moved >= size, moved - size, moved)
 
 
 def places():
     g, s = lax.axis_index("grp"), lax.axis_index("sp")
-    x, z_lo, c = lax.div(g, 8), lax.rem(lax.div(g, 2), 4), lax.rem(g, 2)
-    y, z_hi = lax.div(s, 2), lax.rem(s, 2)
+    x, z_lo, c = g // 8, (g // 2) % 4, g % 2
+    y, z_hi = s // 2, s % 2
+    plane, column, line = g - 2 * z_lo, s - z_hi, 2 * z_lo
 
     def along_z(z):
-        return (x * 8 + lax.rem(z, 4) * 2 + c, y * 2 + lax.div(z, 4))
+        high = (z >= 4).astype(jnp.int32)
+        return (plane + 2 * (z - 4 * high), column + high)
 
     def along_y(at):
         return (g, at * 2 + z_hi)
 
     def along_xc(at):
-        return (lax.div(at, 2) * 8 + z_lo * 2 + lax.rem(at, 2), s)
-
-    return ((z_hi * 4 + z_lo, along_z), (y, along_y), (x * 2 + c, along_xc))
+        core = (at >= 4).astype(jnp.int32)
+        return ((at - 4 * core) * 8 + line + core, s)
+
+    return ((z_hi * 4 + z_lo, along_z), (y, along_y), (c * 4 + x, along_xc))
+
+
+def steps(side):
+    return sorted(range(1, side), key=lambda step: -min(step, side - step))
 
 
 def contract(a, b, dims):
@@ -54,7 +60,8 @@
     q_in, g_in, k_in, v_in, gains, doc, length,
     k_halo, v_halo, doc_halo,
     qn, xhat, rfac, kn, kxhat, krfac, bias, live,
-    dq, dk_own, dv_own, k_send, v_send, k_back, v_back, gq_stage,
+    w_own, g_own, own_high, own_sum, own_delta,
+    dq, gq_sum, gk_sum, dk_own, dv_own, k_send, v_send, k_back, v_back, gq_stage,
     ar_send, ar_recv,
     in_sem, fwd_send, fwd_recv, ret_send, ret_recv, ars_sem, arr_sem, out_sem,
 ):
@@ -79,9 +86,13 @@
         greet(prv)
 
     rows = places()
-    for here, device in rows:
-        for step in (4, 3, 5, 2, 6, 1, 7):
-            greet(device(ring(here, step, SIDE)))
+    peers = [
+        {step: device(ring(here, step, side)) for step in steps(side)}
+        for (here, device), side in zip(rows, SIDES)
+    ]
+    for row in peers:
+        for d in row.values():
+            greet(d)
 
     loads = [
         (k_hbm, k_in), (v_hbm, v_in), (doc_hbm, doc), (len_hbm, length),
@@ -93,11 +104,16 @@
         loads.append((q_hbm.at[:, cols], q_in.at[:, cols]))
         loads.append((g_hbm.at[:, cols], g_in.at[:, cols]))
     loads = [pltpu.make_async_copy(s, d, in_sem.at[i]) for i, (s, d) in enumerate(loads)]
-    for cp in loads:
-        cp.start()
+
+    def head_cols(c):
+        return pl.ds(pl.multiple_of(c * T, T), T)
+
+    def start_loads():
+        for cp in loads:
+            cp.start()
 
     def forward(c):
-        cols = pl.ds(c * T, T)
+        cols = head_cols(c)
         return (
             pltpu.make_async_remote_copy(
                 k_hbm.at[:, cols], k_halo.at[:, cols], fwd_send.at[2 * c], fwd_recv.at[2 * c],
@@ -117,7 +133,7 @@
 
     def open_and_send():
         near = has_next.astype(jnp.int32) + has_prev.astype(jnp.int32)
-        pl.semaphore_wait(barrier, STAGES * (SIDE - 1) + near)
+        pl.semaphore_wait(barrier, sum(SIDES) - len(SIDES) + near)
 
         @pl.when(has_next)
         def _():
@@ -129,6 +145,11 @@
     @pl.when(jnp.logical_not(early))
     def _():
         open_and_send()
+        start_loads()
+
+    @pl.when(early)
+    def _():
+        start_loads()
 
     for cp in loads[:6]:
         cp.wait()
@@ -138,7 +159,7 @@
         return lax.rsqrt(jnp.mean(x * x, axis=-1, keepdims=True) + eps)
 
     def norm_keys(raw, c, row):
-        x = raw[:, c * T : (c + 1) * T].astype(F32)
+        x = raw[:, head_cols(c)].astype(F32)
         r = factor(x)
         xr = x * r
         kn[c, row : row + T, :] = (xr * gain_k).astype(BF16)
@@ -155,22 +176,41 @@
     place = sp * T + lax.broadcasted_iota(jnp.int32, (1, T), 1)
     live[...] = jnp.where(place < length[...], 1.0, 0.0)
 
-    for c in range(KV):
-        loads[6 + 2 * c].wait()
-        loads[7 + 2 * c].wait()
-
-        def norm_query(i, carry, c=c):
-            h = c * GROUP + i
-            cols = pl.ds(pl.multiple_of(h * T, T), T)
-            x = q_in[:, cols].astype(F32)
-            r = factor(x)
-            xr = x * r
-            qn[h] = (xr * gain_q).astype(BF16)
-            xhat[h] = xr
-            rfac[h] = jnp.broadcast_to(r, (T, T))
-            return carry
-
-        lax.fori_loop(0, GROUP, norm_query, 0, unroll=4)
+    own_bias = jnp.concatenate([bias[T:, :], bias[T:, :]], axis=1)
+
+    def load_grad(h):
+        col0 = pl.ds(pl.multiple_of(h * T, T), T)
+        col1 = pl.ds(pl.multiple_of(h * T + T, T), T)
+        return jnp.concatenate([g_in[:, col0], g_in[:, col1]], axis=0)
+
+    def own_block(c, carry):
+        group = pl.ds(pl.multiple_of(c * wide, wide), wide)
+        for k, (src, dst) in enumerate(((q_hbm, q_in), (g_hbm, g_in))):
+            pltpu.make_async_copy(src.at[:, group], dst.at[:, group], in_sem.at[6 + 2 * c + k]).wait()
+        own_key = kn[c, T:, :]
+        own_value = v_in[:, head_cols(c)]
+        for i in range(GROUP // 2):
+            p = c * (GROUP // 2) + i
+            for h in (2 * p, 2 * p + 1):
+                x = q_in[:, head_cols(h)].astype(F32)
+                r = factor(x)
+                xr = x * r
+                qn[h] = (xr * gain_q).astype(BF16)
+                xhat[h] = xr
+                rfac[h] = jnp.broadcast_to(r, (T, T))
+            query = jnp.concatenate([qn[2 * p], qn[2 * p + 1]], axis=0)
+            score = contract(own_key, query, ((1,), (1,))) + own_bias
+            high = jnp.max(score, axis=0, keepdims=True)
+            weight = jnp.exp((score - high) * scale)
+            gatt = contract(own_value, load_grad(2 * p), ((1,), (1,)))
+            w_own[p] = weight
+            g_own[p] = gatt
+            own_high[p] = high
+            own_sum[p] = jnp.sum(weight, axis=0, keepdims=True)
+            own_delta[p] = jnp.sum(weight * gatt, axis=0, keepdims=True)
+        return carry
+
+    lax.fori_loop(0, KV, own_block, 0)
 
     @pl.when(early)
     def _():
@@ -191,7 +231,7 @@
     bias[:T, :] = jnp.where(doc_s == doc_t, first, masked_score)
 
     def back(c):
-        cols = pl.ds(c * T, T)
+        cols = head_cols(c)
         return (
             pltpu.make_async_remote_copy(
                 k_send.at[:, cols], k_back.at[:, cols], ret_send.at[2 * c], ret_recv.at[2 * c],
@@ -203,142 +243,155 @@
             ),
         )
 
-    gain_q_sum = jnp.zeros((T, T), F32)
-    gain_k_sum = jnp.zeros((2 * T, T), F32)
-    for c in range(KV):
-        cols = slice(c * T, (c + 1) * T)
+    far_bias = jnp.concatenate([bias[:T, :], bias[:T, :]], axis=1)
+    alive = jnp.concatenate([live[...], live[...]], axis=1)
+    gq_sum[...] = jnp.zeros_like(gq_sum)
+    gk_sum[...] = jnp.zeros_like(gk_sum)
+
+    def block(c, carry):
+        cols = head_cols(c)
 
         @pl.when(has_prev)
-        def _(c=c):
+        def _():
             for cp in forward(c):
                 cp.wait_recv()
 
         norm_keys(k_halo, c, 0)
         key = kn[c]
-        value = jnp.concatenate([v_halo[:, cols], v_in[:, cols]], axis=0)
-
-        def pair(i, carry, c=c, key=key, value=value):
-            dk, dv, gq_sum = carry
-            h = c * GROUP + 2 * i
+        value = v_halo[:, cols]
+        ds_all, att_all, grads, gains_here = [], [], [], []
+        for i in range(GROUP // 2):
+            p = c * (GROUP // 2) + i
+            h = 2 * p
             query = jnp.concatenate([qn[h], qn[h + 1]], axis=0)
-            col0 = pl.ds(pl.multiple_of(h * T, T), T)
-            col1 = pl.ds(pl.multiple_of(h * T + T, T), T)
-            grad = jnp.concatenate([g_in[:, col0], g_in[:, col1]], axis=0)
-            both = jnp.concatenate([bias[...], bias[...]], axis=1)
-            score = contract(key, query, ((1,), (1,))) + both
-            high = jnp.max(score, axis=0, keepdims=True)
+            grad = load_grad(h)
+            score = contract(key[:T], query, ((1,), (1,))) + far_bias
+            high = jnp.maximum(own_high[p], jnp.max(score, axis=0, keepdims=True))
             weight = jnp.exp((score - high) * scale)
-            total = jnp.sum(weight, axis=0, keepdims=True)
-            alive = jnp.concatenate([live[...], live[...]], axis=1)
-            att = weight * (alive / total)
+            shrink = jnp.exp((own_high[p] - high) * scale)
+            total = shrink * own_sum[p] + jnp.sum(weight, axis=0, keepdims=True)
+            inverse = alive / total
             gatt = contract(value, grad, ((1,), (1,)))
-            delta = jnp.sum(att * gatt, axis=0, keepdims=True)
-            ds = (att * (gatt - delta)).astype(BF16)
-            dk = dk + contract(ds, query, ((1,), (0,)))
-            dv = dv + contract(att.astype(BF16), grad, ((1,), (0,)))
+            delta = shrink * own_delta[p] + jnp.sum(weight * gatt, axis=0, keepdims=True)
+            delta = delta * inverse
+            far = weight * inverse
+            near = w_own[p] * (shrink * inverse)
+            far_ds = (far * (gatt - delta)).astype(BF16)
+            near_ds = (near * (g_own[p] - delta)).astype(BF16)
+            ds = jnp.concatenate([far_ds, near_ds], axis=0)
+            ds_all.append(ds)
+            att_all.append(jnp.concatenate([far.astype(BF16), near.astype(BF16)], axis=0))
+            grads.append(grad)
             dq2 = contract(ds, key, ((0,), (0,))) * scale
             dq[h] = dq2[:T]
             dq[h + 1] = dq2[T:]
-            gq_sum = gq_sum + dq2[:T] * xhat[h] + dq2[T:] * xhat[h + 1]
-            return dk, dv, gq_sum
-
-        zero = jnp.zeros((2 * T, T), F32)
-        dk, dv, gain_q_sum = lax.fori_loop(0, GROUP // 2, pair, (zero, zero, gain_q_sum), unroll=2)
-        dk = dk * scale
-        gain_k_sum = gain_k_sum + dk * kxhat[c]
+            gains_here.append(dq2[:T] * xhat[h] + dq2[T:] * xhat[h + 1])
+        gq_sum[...] += sum(gains_here[1:], gains_here[0])
+        queries = qn[pl.ds(c * GROUP, GROUP)].reshape(wide, T)
+        dk = contract(jnp.concatenate(ds_all, axis=1), queries, ((1,), (0,))) * scale
+        gk_sum[...] += dk * kxhat[c]
         dk_own[:, cols] = dk[T:]
+        k_send[:, cols] = dk[:T].astype(BF16)
+        dv = contract(jnp.concatenate(att_all, axis=1), jnp.concatenate(grads, axis=0), ((1,), (0,)))
         dv_own[:, cols] = dv[T:]
-        k_send[:, cols] = dk[:T].astype(BF16)
         v_send[:, cols] = dv[:T].astype(BF16)
-
-        if c < EARLY:
-
-            @pl.when(has_prev)
-            def _(c=c):
-                for cp in back(c):
-                    cp.start()
+        return carry
+
+    lax.fori_loop(0, KV, block, 0)
 
     sums = jnp.concatenate(
         [
-            jnp.sum(gain_q_sum, axis=0, keepdims=True),
-            jnp.sum(gain_k_sum, axis=0, keepdims=True),
+            jnp.sum(gq_sum[...], axis=0, keepdims=True),
+            jnp.sum(gk_sum[...], axis=0, keepdims=True),
         ],
         axis=0,
     )
 
     def exchange(stage):
-        here, device = rows[stage]
+        (here, _), side = rows[stage], SIDES[stage]
+        base = sum(SIDES[:stage])
         return [
             pltpu.make_async_remote_copy(
-                ar_send.at[stage], ar_recv.at[stage, here], ars_sem.at[stage, step - 1],
-                arr_sem.at[stage, here], device_id=device(ring(here, step, SIDE)),
+                ar_send.at[stage], ar_recv.at[base + here], ars_sem.at[base + step],
+                arr_sem.at[base + here], device_id=peers[stage][step],
                 device_id_type=MESH,
             )
-            for step in (4, 3, 5, 2, 6, 1, 7)
+            for step in steps(side)
         ]
 
     def send_sums(stage, sums):
         ar_send[stage] = sums
-        ar_recv[stage, rows[stage][0]] = sums
         for cp in exchange(stage):
             cp.start()
+        ar_recv[sum(SIDES[:stage]) + rows[stage][0]] = sums
 
     def gather_sums(stage):
-        here, _ = rows[stage]
-        for step in range(1, SIDE):
-            at = ring(here, step, SIDE)
-            pltpu.make_async_copy(
-                ar_recv.at[stage, at], ar_recv.at[stage, at], arr_sem.at[stage, at]
-            ).wait()
-        total = ar_recv[stage, 0]
-        for at in range(1, SIDE):
-            total = total + ar_recv[stage, at]
+        (here, _), side = rows[stage], SIDES[stage]
+        base = sum(SIDES[:stage])
+        for step in range(1, side):
+            at = base + ring(here, step, side)
+            pltpu.make_async_copy(ar_recv.at[at], ar_recv.at[at], arr_sem.at[at]).wait()
+        total = ar_recv[base]
+        for at in range(1, side):
+            total = total + ar_recv[base + at]
         return total
 
     send_sums(0, sums)
 
-    @pl.when(has_prev)
-    def _():
-        for c in range(EARLY, KV):
+    row = rows[0][0]
+    last_in = (row == 5) | (row == 6)
+
+    def start_back():
+        for c in range(KV):
             for cp in back(c):
                 cp.start()
+
+    @pl.when(has_prev & last_in)
+    def _():
+        start_back()
 
     def backward(xr, r, gain, up):
         u = gain * up
         return r * (u - xr * jnp.mean(u * xr, axis=-1, keepdims=True))
 
-    writes = []
-    for c in range(KV):
-
-        def query_grad(i, carry, c=c):
+    def result(c):
+        cols = pl.ds(pl.multiple_of(c * wide, wide), wide)
+        return pltpu.make_async_copy(gq_stage.at[:, cols], gq_out.at[:, cols], out_sem.at[c])
+
+    def query_grads(c, carry):
+        for i in range(GROUP):
             h = c * GROUP + i
-            cols = pl.ds(pl.multiple_of(h * T, T), T)
-            gq_stage[:, cols] = backward(xhat[h], rfac[h], gain_q, dq[h]).astype(BF16)
-            return carry
-
-        lax.fori_loop(0, GROUP, query_grad, 0, unroll=4)
-        cols = pl.ds(c * wide, wide)
-        cp = pltpu.make_async_copy(gq_stage.at[:, cols], gq_out.at[:, cols], out_sem.at[c])
-        cp.start()
-        writes.append(cp)
+            up = backward(xhat[h], rfac[h], gain_q, dq[h])
+            gq_stage[:, head_cols(h)] = up.astype(BF16)
+        result(c).start()
+        return carry
+
+    lax.fori_loop(0, KV, query_grads, 0)
 
     send_sums(1, gather_sums(0))
 
+    @pl.when(has_prev & jnp.logical_not(last_in))
+    def _():
+        start_back()
+
     send_sums(2, gather_sums(1))
 
-    for c in range(KV):
-        cols = slice(c * T, (c + 1) * T)
+    def finish(c, carry):
+        cols = head_cols(c)
 
         @pl.when(has_next)
-        def _(c=c, cols=cols):
+        def _():
             for cp in back(c):
                 cp.wait_recv()
             dk_own[:, cols] = dk_own[:, cols] + k_back[:, cols].astype(F32)
             dv_own[:, cols] = dv_own[:, cols] + v_back[:, cols].astype(F32)
 
-        gk_out[:, cols] = backward(kxhat[c, T:, :], krfac[c], gain_k, dk_own[:, cols]).astype(BF16)
+        up = backward(kxhat[c, T:, :], krfac[c], gain_k, dk_own[:, cols])
+        gk_out[:, cols] = up.astype(BF16)
         gv_out[:, cols] = dv_own[:, cols].astype(BF16)
-
+        return carry
+
+    lax.fori_loop(0, KV, finish, 0)
     gain_out[...] = gather_sums(2) * (1.0 / math.sqrt(T * 512))
 
     @pl.when(has_next)
@@ -354,11 +407,11 @@
             for cp in back(c):
                 cp.wait_send()
 
-    for stage in range(STAGES):
+    for stage in range(len(SIDES)):
         for cp in exchange(stage):
             cp.wait_send()
-    for cp in writes:
-        cp.wait()
+    for c in range(KV):
+        result(c).wait()
 
 
 def hand_over(gq, gk, gv, gain, gq_out, gk_out, gv_out, gain_q_out, gain_k_out, wide, near, last, sem):
@@ -407,14 +460,17 @@
             pltpu.VMEM((KV, 2 * T, T), BF16), pltpu.VMEM((KV, 2 * T, T), F32),
             pltpu.VMEM((KV, T, T), F32),
             pltpu.VMEM((2 * T, T), F32), pltpu.VMEM((1, T), F32),
-            pltpu.VMEM((HEADS, T, T), F32),
+            pltpu.VMEM((HEADS // 2, T, 2 * T), F32), pltpu.VMEM((HEADS // 2, T, 2 * T), F32),
+            pltpu.VMEM((HEADS // 2, 1, 2 * T), F32), pltpu.VMEM((HEADS // 2, 1, 2 * T), F32),
+            pltpu.VMEM((HEADS // 2, 1, 2 * T), F32),
+            pltpu.VMEM((HEADS, T, T), F32), pltpu.VMEM((T, T), F32), pltpu.VMEM((2 * T, T), F32),
             pltpu.VMEM(narrow, F32), pltpu.VMEM(narrow, F32),
             pltpu.VMEM(narrow, BF16), pltpu.VMEM(narrow, BF16),
             pltpu.VMEM(narrow, BF16), pltpu.VMEM(narrow, BF16),
             pltpu.VMEM(wide, BF16),
-            pltpu.VMEM((STAGES, 2, T), F32), pltpu.VMEM((STAGES, SIDE, 2, T), F32),
+            pltpu.VMEM((len(SIDES), 2, T), F32), pltpu.VMEM((sum(SIDES), 2, T), F32),
             dma((14,)), dma((9,)), dma((9,)), dma((8,)), dma((8,)),
-            dma((STAGES, SIDE - 1)), dma((STAGES, SIDE)), dma((KV,)),
+            dma((sum(SIDES),)), dma((sum(SIDES),)), dma((KV,)),
         ],
         compiler_params=pltpu.CompilerParams(
             collective_id=0, has_side_effects=True, vmem_limit_bytes=60 * 2**20

time: 52.2 us -> 50.3 us (0.964)
  the two profiles are of different devices: /device:TPU:1 before, /device:TPU:48 now
where the time goes in v3:
time: 50.3 us; the launch traced here: 50.1 us
  Pallas kernels  48.9 us (97%)
  between operations  1.29 us (3%)
    pallas_call x1, Pallas kernels, body(): pl.pallas_call(kernel, out_shape=(jax.ShapeDtypeStruct(wide, BF16), jax.S...  46.7 us
    pallas_call x1, Pallas kernels, body(): pl.pallas_call(hand_over, out_shape=(jax.ShapeDtypeStruct(wide, BF16), ja...  2.2 us

profile of v3, /device:TPU:48, one launch (start us, length us, event | category | flops | bytes accessed | tf_op | source)
XLA Modules:
  0.0 50.1 jit_solution(3550385749014682531)
XLA Ops:
  1.3 46.7 %shard_map.119 = (bf16[128,4096]{1,0:T(8,128)(2,1)}, bf16[128,512]{1,0:T(8,128)(2,1)}, bf16[128,512]{1,0:T(8,128)(2,1)}, f32[2,128]{1,0:T(2,128)}) custom-call(bf16[128,4096]{1,0:T(8,128)(2,1)} %q_hbm.1, bf16[128,512]{1,0:T(8,128)(2,1)} %k_hbm.1, bf16[128,512]{1,0:T(8,128)(2,1)} %v_hbm.1, bf16[128,4096]{1,0:T(8,128)(2,1)} %g_hbm.1, f32[1,128]{1,0:T(1,128)} %bitcast.7, ...), custom_call_target="tpu_custom_call" | custom-call | tf_op jit(solution)/shard_map/pallas_call | solution.py:443
  48.0 2.2 %shard_map.120 = (bf16[128,4096]{1,0:T(8,128)(2,1)}, bf16[128,512]{1,0:T(8,128)(2,1)}, bf16[128,512]{1,0:T(8,128)(2,1)}, f32[1,128]{1,0:T(1,128)}, f32[1,128]{1,0:T(1,128)}) custom-call(bf16[128,4096]{1,0:T(8,128)(2,1)} %get-tuple-element.14.gq, bf16[128,512]{1,0:T(8,128)(2,1)} %get-tuple-element.15.gk, bf16[128,512]{1,0:T(8,128)(2,1)} %get-tuple-element.16.gv, ...), custom_call_target="tpu_custom_call" | custom-call | tf_op jit(solution)/shard_map/pallas_call | solution.py:482

commit v4 on v3

--- a/solution.py
+++ b/solution.py
@@ -61,7 +61,7 @@
     k_halo, v_halo, doc_halo,
     qn, xhat, rfac, kn, kxhat, krfac, bias, live,
     w_own, g_own, own_high, own_sum, own_delta,
-    dq, gq_sum, gk_sum, dk_own, dv_own, k_send, v_send, k_back, v_back, gq_stage,
+    att_low, dq, gq_sum, gk_sum, dk_own, dv_own, k_send, v_send, k_back, v_back, gq_stage,
     ar_send, ar_recv,
     in_sem, fwd_send, fwd_recv, ret_send, ret_recv, ars_sem, arr_sem, out_sem,
 ):
@@ -259,7 +259,7 @@
         norm_keys(k_halo, c, 0)
         key = kn[c]
         value = v_halo[:, cols]
-        ds_all, att_all, grads, gains_here = [], [], [], []
+        ds_all, att_all, gains_here = [], [], []
         for i in range(GROUP // 2):
             p = c * (GROUP // 2) + i
             h = 2 * p
@@ -281,7 +281,6 @@
             ds = jnp.concatenate([far_ds, near_ds], axis=0)
             ds_all.append(ds)
             att_all.append(jnp.concatenate([far.astype(BF16), near.astype(BF16)], axis=0))
-            grads.append(grad)
             dq2 = contract(ds, key, ((0,), (0,))) * scale
             dq[h] = dq2[:T]
             dq[h + 1] = dq2[T:]
@@ -292,12 +291,18 @@
         gk_sum[...] += dk * kxhat[c]
         dk_own[:, cols] = dk[T:]
         k_send[:, cols] = dk[:T].astype(BF16)
-        dv = contract(jnp.concatenate(att_all, axis=1), jnp.concatenate(grads, axis=0), ((1,), (0,)))
+        att_low[c] = jnp.concatenate(att_all, axis=1)
+        return carry
+
+    lax.fori_loop(0, KV, block, 0)
+
+    def value_sums(c, carry):
+        cols = head_cols(c)
+        grads = jnp.concatenate([g_in[:, head_cols(c * GROUP + i)] for i in range(GROUP)], axis=0)
+        dv = contract(att_low[c], grads, ((1,), (0,)))
         dv_own[:, cols] = dv[T:]
         v_send[:, cols] = dv[:T].astype(BF16)
         return carry
-
-    lax.fori_loop(0, KV, block, 0)
 
     sums = jnp.concatenate(
         [
@@ -337,6 +342,7 @@
         return total
 
     send_sums(0, sums)
+    lax.fori_loop(0, KV, value_sums, 0)
 
     row = rows[0][0]
     last_in = (row == 5) | (row == 6)
@@ -463,6 +469,7 @@
             pltpu.VMEM((HEADS // 2, T, 2 * T), F32), pltpu.VMEM((HEADS // 2, T, 2 * T), F32),
             pltpu.VMEM((HEADS // 2, 1, 2 * T), F32), pltpu.VMEM((HEADS // 2, 1, 2 * T), F32),
             pltpu.VMEM((HEADS // 2, 1, 2 * T), F32),
+            pltpu.VMEM((KV, 2 * T, GROUP * T), BF16),
             pltpu.VMEM((HEADS, T, T), F32), pltpu.VMEM((T, T), F32), pltpu.VMEM((2 * T, T), F32),
             pltpu.VMEM(narrow, F32), pltpu.VMEM(narrow, F32),
             pltpu.VMEM(narrow, BF16), pltpu.VMEM(narrow, BF16),

time: 50.3 us -> 50 us (level)
  no operation moved by 1% of the time
where the time goes in v4:
time: 50 us; the launch traced here: 49.8 us
  Pallas kernels  48.6 us (97%)
  between operations  1.29 us (3%)
    pallas_call x1, Pallas kernels, body(): pl.pallas_call(kernel, out_shape=(jax.ShapeDtypeStruct(wide, BF16), jax.S...  46.4 us
    pallas_call x1, Pallas kernels, body(): pl.pallas_call(hand_over, out_shape=(jax.ShapeDtypeStruct(wide, BF16), ja...  2.2 us

profile of v4, /device:TPU:48, one launch (start us, length us, event | category | flops | bytes accessed | tf_op | source)
XLA Modules:
  0.0 49.8 jit_solution(16896000709342182976)
XLA Ops:
  1.3 46.4 %shard_map.119 = (bf16[128,4096]{1,0:T(8,128)(2,1)}, bf16[128,512]{1,0:T(8,128)(2,1)}, bf16[128,512]{1,0:T(8,128)(2,1)}, f32[2,128]{1,0:T(2,128)}) custom-call(bf16[128,4096]{1,0:T(8,128)(2,1)} %q_hbm.1, bf16[128,512]{1,0:T(8,128)(2,1)} %k_hbm.1, bf16[128,512]{1,0:T(8,128)(2,1)} %v_hbm.1, bf16[128,4096]{1,0:T(8,128)(2,1)} %g_hbm.1, f32[1,128]{1,0:T(1,128)} %bitcast.7, ...), custom_call_target="tpu_custom_call" | custom-call | tf_op jit(solution)/shard_map/pallas_call | solution.py:449
  47.7 2.2 %shard_map.120 = (bf16[128,4096]{1,0:T(8,128)(2,1)}, bf16[128,512]{1,0:T(8,128)(2,1)}, bf16[128,512]{1,0:T(8,128)(2,1)}, f32[1,128]{1,0:T(1,128)}, f32[1,128]{1,0:T(1,128)}) custom-call(bf16[128,4096]{1,0:T(8,128)(2,1)} %get-tuple-element.14.gq, bf16[128,512]{1,0:T(8,128)(2,1)} %get-tuple-element.15.gk, bf16[128,512]{1,0:T(8,128)(2,1)} %get-tuple-element.16.gv, ...), custom_call_target="tpu_custom_call" | custom-call | tf_op jit(solution)/shard_map/pallas_call | solution.py:489

commit v5 on v4

--- a/solution.py
+++ b/solution.py
@@ -342,7 +342,6 @@
         return total
 
     send_sums(0, sums)
-    lax.fori_loop(0, KV, value_sums, 0)
 
     row = rows[0][0]
     last_in = (row == 5) | (row == 6)
@@ -352,9 +351,19 @@
             for cp in back(c):
                 cp.start()
 
+    def start_part(part):
+        for c in range(KV):
+            back(c)[part].start()
+
     @pl.when(has_prev & last_in)
     def _():
-        start_back()
+        start_part(0)
+
+    lax.fori_loop(0, KV, value_sums, 0)
+
+    @pl.when(has_prev & last_in)
+    def _():
+        start_part(1)
 
     def backward(xr, r, gain, up):
         u = gain * up

time: 50 us -> 50.2 us (level)
  no operation moved by 1% of the time
where the time goes in v5:
time: 50.2 us; the launch traced here: 50 us
  Pallas kernels  48.7 us (97%)
  between operations  1.29 us (3%)
    pallas_call x1, Pallas kernels, body(): pl.pallas_call(kernel, out_shape=(jax.ShapeDtypeStruct(wide, BF16), jax.S...  46.5 us
    pallas_call x1, Pallas kernels, body(): pl.pallas_call(hand_over, out_shape=(jax.ShapeDtypeStruct(wide, BF16), ja...  2.2 us

profile of v5, /device:TPU:48, one launch (start us, length us, event | category | flops | bytes accessed | tf_op | source)
XLA Modules:
  0.0 50.0 jit_solution(5983362579686781280)
XLA Ops:
  1.3 46.5 %shard_map.119 = (bf16[128,4096]{1,0:T(8,128)(2,1)}, bf16[128,512]{1,0:T(8,128)(2,1)}, bf16[128,512]{1,0:T(8,128)(2,1)}, f32[2,128]{1,0:T(2,128)}) custom-call(bf16[128,4096]{1,0:T(8,128)(2,1)} %q_hbm.1, bf16[128,512]{1,0:T(8,128)(2,1)} %k_hbm.1, bf16[128,512]{1,0:T(8,128)(2,1)} %v_hbm.1, bf16[128,4096]{1,0:T(8,128)(2,1)} %g_hbm.1, f32[1,128]{1,0:T(1,128)} %bitcast.7, ...), custom_call_target="tpu_custom_call" | custom-call | tf_op jit(solution)/shard_map/pallas_call | solution.py:458
  47.8 2.2 %shard_map.120 = (bf16[128,4096]{1,0:T(8,128)(2,1)}, bf16[128,512]{1,0:T(8,128)(2,1)}, bf16[128,512]{1,0:T(8,128)(2,1)}, f32[1,128]{1,0:T(1,128)}, f32[1,128]{1,0:T(1,128)}) custom-call(bf16[128,4096]{1,0:T(8,128)(2,1)} %get-tuple-element.14.gq, bf16[128,512]{1,0:T(8,128)(2,1)} %get-tuple-element.15.gk, bf16[128,512]{1,0:T(8,128)(2,1)} %get-tuple-element.16.gv, ...), custom_call_target="tpu_custom_call" | custom-call | tf_op jit(solution)/shard_map/pallas_call | solution.py:498
